TPU v7x, 32 devices: a whole 2x2x4 slice. The times are simulated.
32 devices in a mesh: groups: 2 (over y), vel: 4 (over z), cell: 2 (over x), sub: 2 (over core).
Axes of the slice: x: 2, y: 2, z: 4, core: 2. Of those that a mesh axis runs over, the one named last changes fastest.
Arguments:
- density: bfloat16 [768, 110592], P(('groups', 'cell', 'sub'), 'vel'), parts along dimension 0, may hold values from 0.5 to 1.5
- coder: bfloat16 [110592, 512], P('vel'), may hold values from -0.01953125 to 0.01953125
- w_latent: bfloat16 [512, 512], replicated, may hold values from -0.25 to 0.25
- b_latent: float32 [512], replicated, may hold values from -3 to 3
- restitution: float32 [768], P(('groups', 'cell', 'sub')), parts along dimension 0, may hold values from 0.3 to 0.95
- inflow: float32 [221184], P(('groups', 'vel')), parts along dimension 0, may hold values from 0.5 to 1.5
- flags: int32 [8], P('groups'), parts along dimension 0, may hold values from 0 to 1, as said below
- blocks: int32 [192], P(('groups', 'vel')), parts along dimension 0, may hold values from 0 to 95, each once
Outputs:
- density_out: bfloat16 [768, 110592], P(('groups', 'cell', 'sub'), 'vel'), parts along dimension 0
There are 2 independent parts, one for each index of `groups`. A program takes and returns all parts, laid end to end along the dimension named above; an argument that names none is the same for every part. Nothing has to cross between parts.
Inputs may be any that keep to these rules, and one draw needn't show every extreme that they name: flags[b] = 1 joins block b of 96 cells to block b - 1 (block 0 to the last block); 0 makes that boundary an inflow boundary. Every draw holds both values. A permutation of the velocity blocks.
All inputs are finite; a program needn't handle non-finite values.
Results may differ from a plain program's by a relative error of at most 0.007.
Values may be sent and summed in bfloat16 or wider, within the bound.
A program may use at most 128 MiB of HBM per device.

v0:
```python
import math

import jax
import jax.numpy as jnp
import numpy as np
from jax import lax
from jax.sharding import PartitionSpec as P

VGRID = 48
LATENT = 512
VBLOCKS = 96
STEPS = 2
VELS = 110592


SINK_RATE = 0.5
COURANT = 0.9


def extended(cells, sides, width):
    for axis, dim in sides:
        count = lax.axis_size(axis)
        head = lax.slice_in_dim(cells, 0, width, axis=dim)
        tail = lax.slice_in_dim(cells, cells.shape[dim] - width, cells.shape[dim], axis=dim)
        cells = jnp.concatenate(
            [
                lax.ppermute(tail, axis, [(i, (i + 1) % count) for i in range(count)]),
                cells,
                lax.ppermute(head, axis, [((i + 1) % count, i) for i in range(count)]),
            ],
            axis=dim,
        )
    return cells


def grid_moments():
    centres = (2.0 * np.arange(VGRID) + 1.0 - VGRID) / VGRID
    second = float(np.sum(centres**2))
    fourth = float(np.sum(centres**4))
    number = float(VGRID)
    total = number**3
    cross = 3.0 * number * number * second
    quartic = 3.0 * number * number * fourth + 6.0 * number * second * second
    square = number * number * second
    return (total, cross, quartic, square)


def component(number):
    return (2 * number + 1 - VGRID).astype(jnp.float32) / VGRID


def velocity_rows(blocks):
    width = VELS // VBLOCKS
    number = (blocks[:, None] * width + jnp.arange(width, dtype=jnp.int32)[None, :]).reshape(-1)
    along_x = component(number // (VGRID * VGRID))
    along_y = component(number // VGRID % VGRID)
    along_z = component(number % VGRID)
    kinetic = along_x * along_x + along_y * along_y + along_z * along_z
    return jnp.stack([jnp.ones_like(along_x), along_x, along_y, along_z, kinetic])


def advect(padded, courant):
    length = padded.shape[0] - 4
    magnitude = jnp.abs(courant)
    lower = padded[0 : length + 1]
    centre = padded[1 : length + 2]
    upper = padded[2 : length + 3]
    beyond = padded[3 : length + 4]
    upwind = (1.0 - magnitude) / 2.0
    curved = (1.0 - magnitude * magnitude) / 6.0
    forward = centre + upwind * (upper - centre) - curved * (upper - 2.0 * centre + lower)
    backward = upper + upwind * (centre - upper) - curved * (centre - 2.0 * upper + beyond)
    flux = courant * jnp.where(courant >= 0.0, forward, backward)
    return padded[2 : length + 2] - (flux[1:] - flux[:-1])


def project(fstar, collision, moments, energy_sum, restitution, basis):
    total, cross, quartic, square = grid_moments()
    sink = -SINK_RATE * (1.0 - restitution * restitution) * energy_sum
    excess = moments[4] - sink
    determinant = total * quartic - cross * cross
    mass_mult = (quartic * moments[0] - cross * excess) / determinant
    energy_mult = (total * excess - cross * moments[0]) / determinant
    weights = jnp.stack(
        [mass_mult, moments[1] / square, moments[2] / square, moments[3] / square, energy_mult]
    )
    correction = lax.dot_general(
        weights, basis, (((0,), (0,)), ((), ())), precision=lax.Precision.HIGHEST
    )
    return fstar + (collision - correction)


def latent_layer(encoded, w_latent, b_latent):
    mixed = jnp.dot(encoded.astype(jnp.bfloat16), w_latent, preferred_element_type=jnp.float32)
    return jnp.tanh(mixed + b_latent).astype(jnp.bfloat16)


def body(density, coder, w_latent, b_latent, restitution, inflow, flags, blocks):
    basis = velocity_rows(blocks)
    courant = COURANT * basis[1]
    sub_count = lax.axis_size("sub")
    position = lax.axis_index("cell") * sub_count + lax.axis_index("sub")
    block_count = lax.axis_size("cell") * sub_count
    open_left = lax.dynamic_index_in_dim(flags, position, 0, keepdims=False) == 1
    open_right = (
        lax.dynamic_index_in_dim(flags, (position + 1) % block_count, 0, keepdims=False) == 1
    )
    scale = math.sqrt(VELS / LATENT)
    state = density.astype(jnp.float32)
    for section_index in range(STEPS):
        padded = extended(state, ((("cell", "sub"), 0),), 2)
        lead_rows = jnp.where(open_left, padded[:2], inflow[None, :])
        tail_rows = jnp.where(open_right, padded[-2:], inflow[None, :])
        padded = jnp.concatenate([lead_rows, padded[2:-2], tail_rows], 0)
        fstar = advect(padded, courant)
        coarse = fstar.astype(jnp.bfloat16)
        partial_code = jnp.dot(coarse, coder, preferred_element_type=jnp.float32)
        partial_energy = jnp.dot(fstar, basis[4], precision=lax.Precision.HIGHEST)
        encoded, energy_sum = lax.psum((partial_code, partial_energy), "vel")
        active = latent_layer(encoded, w_latent, b_latent)
        collision = scale * lax.dot_general(
            active, coder, (((1,), (1,)), ((), ())), preferred_element_type=jnp.float32
        )
        local_part = lax.dot_general(
            basis, collision, (((1,), (1,)), ((), ())), precision=lax.Precision.HIGHEST
        )
        moments = lax.psum(local_part, "vel")
        state = project(fstar, collision, moments, energy_sum, restitution, basis)
    return state.astype(jnp.bfloat16)


def solution(mesh):
    return jax.shard_map(
        body,
        mesh=mesh,
        in_specs=(
            P(("groups", "cell", "sub"), "vel"),
            P("vel", None),
            P(),
            P(),
            P(("groups", "cell", "sub")),
            P(("groups", "vel")),
            P("groups"),
            P(("groups", "vel")),
        ),
        out_specs=P(("groups", "cell", "sub"), "vel"),
        check_vma=False,
    )
```

profile of v0, /device:TPU:0, one launch (start us, length us, event | category | flops | bytes accessed | tf_op | source)
XLA Modules:
  0.0 265.1 jit_solution(6619362317704256406)
XLA Ops:
  1.9 2.0 collective-permute-start.1
  7.4 7.5 %convert_element_type.81 = f32[96,27648]{1,0:T(8,128)} convert(bf16[96,27648]{1,0:T(8,128)(2,1)} %param.8) | non-fusion elementwise | flops 2654208 | bytes 15925248 | tf_op jit(solution)/shard_map/convert_element_type | solution.py:109
  18.2 18.1 %fusion.15 = f32[97,27648]{1,0:T(8,128)S(1)} fusion(f32[2,27648]{1,0:T(2,128)S(1)} %get-tuple-element.28, f32[96,27648]{1,0:T(8,128)} %convert_element_type.81, f32[2,27648]{1,0:T(2,128)S(1)} %get-tuple-element.27, f32[27648]{0:T(1024)S(1)} %get-tuple-element.26, f32[27648]{0:T(1024)S(1)} %get-tuple-element.25, f32[27648]{0:T(1024)S(1)} %get-tuple-element.18, ...), kind=kLoop, calls=%fused_computation.24 | loop fusion | flops 59000832 | bytes 22146048 | tf_op jit(solution)/shard_map/mul | solution.py:73
  36.3 1.8 fusion.20
  38.1 4.0 %copy-done.1 = f32[96,27648]{1,0:T(8,128)} copy-done((f32[96,27648]{1,0:T(8,128)}, f32[96,27648]{1,0:T(8,128)S(1)}, u32[]{:S(2)}) %copy-start.1) | copy-done | bytes 10616856
  42.2 8.3 %convolution_bitcast_fusion.1 = f32[96]{0:T(128)S(1)} fusion(f32[96,27648]{1,0:T(8,128)S(1)} %fusion.20, f32[27648,1]{0,1:T(1,128)S(1)} %bitcast.88), kind=kOutput, calls=%fused_computation.46 | convolution fusion | flops 31850496 | bytes 10727808 | tf_op jit(solution)/shard_map/dot_general | solution.py:118
  50.5 14.5 %fusion.23 = f32[96,512]{1,0:T(8,128)S(1)} fusion(bf16[27648,512]{1,0:T(8,128)(2,1)} %param.9, f32[96,27648]{1,0:T(8,128)} %copy-done.1), kind=kOutput, calls=%fused_computation.37 | convolution fusion | flops 2720563200 | bytes 39124992 | tf_op jit(solution)/shard_map/dot_general | solution.py:117
  65.0 23.8 %all-reduce.4 = bf16[96,512]{1,0:T(8,128)(2,1)S(1)} all-reduce(f32[96,512]{1,0:T(8,128)S(1)} %fusion.23), channel_id=1, replica_groups=mesh['groups'=2,'vel'=4,'cell'=2,'sub'=2] {'vel'}, use_global_device_ids=true, to_apply=%region_0.1 | all-reduce | flops 49152 | bytes 294912 | tf_op jit(solution)/shard_map/psum | solution.py:119
  88.8 17.9 %convolution_multiply_fusion.1 = f32[96,27648]{1,0:T(8,128)} fusion(bf16[27648,512]{1,0:T(8,128)(2,1)} %param.9, bf16[512,512]{1,0:T(8,128)(2,1)S(1)} %copy-done, f32[512]{0:T(512)S(1)} %copy-done.4, bf16[96,512]{1,0:T(8,128)(2,1)S(1)} %all-reduce.4), kind=kOutput, calls=%fused_computation.1 | convolution fusion | flops 2770993152 | bytes 39553024 | tf_op jit(solution)/shard_map/dot_general | solution.py:121
  106.7 10.9 %fusion.82 = f32[5,96]{1,0:T(8,128)S(1)} fusion(f32[5,27648]{1,0:T(8,128)S(1)} %stack.14, f32[96,27648]{1,0:T(8,128)} %convolution_multiply_fusion.1), kind=kOutput, calls=%fused_computation.129 | convolution fusion | flops 159252480 | bytes 11171712 | tf_op jit(solution)/shard_map/dot_general | solution.py:124
  117.6 8.5 %all-reduce.1 = (f32[96]{0:T(128)S(1)}, f32[5,96]{1,0:T(8,128)S(1)}) all-reduce(f32[96]{0:T(128)S(1)} %convolution_bitcast_fusion.1, f32[5,96]{1,0:T(8,128)S(1)} %fusion.82), channel_id=1, replica_groups=mesh['groups'=2,'vel'=4,'cell'=2,'sub'=2] {'vel'}, use_global_device_ids=true, to_apply=%region_2.3 | all-reduce | flops 576 | bytes 4608 | tf_op jit(solution)/shard_map/psum | solution.py:119
  126.2 12.3 %fusion.1 = f32[96,27648]{1,0:T(8,128)S(1)} fusion(f32[96,27648]{1,0:T(8,128)} %copy-done.1, f32[96,27648]{1,0:T(8,128)} %convolution_multiply_fusion.1, f32[5,96]{1,0:T(8,128)S(1)} %stack.34, f32[5,27648]{1,0:T(8,128)S(1)} %stack.14), kind=kOutput, calls=%fused_computation.5 | convolution fusion | flops 164560896 | bytes 32405376 | tf_op jit(solution)/shard_map/dot_general | solution.py:87
  138.8 1.7 collective-permute-start.3
  140.6 4.5 %collective-permute-done.2 = f32[2,27648]{1,0:T(2,128)S(1)} collective-permute-done((f32[2,27648]{1,0:T(2,128)S(1)}, f32[2,27648]{1,0:T(2,128)S(1)}, u32[]{:S(2)}, u32[]{:S(2)}) %collective-permute-start.2) | collective-permute-done | bytes 221216 | tf_op jit(solution)/shard_map/ppermute | solution.py:27
  145.4 11.2 %fusion.7 = f32[97,27648]{1,0:T(8,128)} fusion(f32[2,27648]{1,0:T(2,128)S(1)} %get-tuple-element.24, f32[96,27648]{1,0:T(8,128)S(1)} %fusion.1, f32[2,27648]{1,0:T(2,128)S(1)} %get-tuple-element.23, f32[27648]{0:T(1024)S(1)} %get-tuple-element.26, f32[27648]{0:T(1024)S(1)} %get-tuple-element.25, f32[27648]{0:T(1024)S(1)} %get-tuple-element.18, ...), kind=kLoop, calls=%fused_computation.12 | loop fusion | flops 59000832 | bytes 22146048 | tf_op jit(solution)/shard_map/mul | solution.py:73
  156.6 8.2 %fusion.19 = f32[96,27648]{1,0:T(8,128)S(1)} fusion(f32[96,27648]{1,0:T(8,128)S(1)} %fusion.1, f32[97,27648]{1,0:T(8,128)} %fusion.7), kind=kLoop, calls=%fused_computation.32 | loop fusion | flops 5308416 | bytes 42467328 | tf_op jit(solution)/shard_map/sub | solution.py:74
  164.8 4.0 %copy-done.2 = f32[96,27648]{1,0:T(8,128)} copy-done((f32[96,27648]{1,0:T(8,128)}, f32[96,27648]{1,0:T(8,128)S(1)}, u32[]{:S(2)}) %copy-start.2) | copy-done | bytes 10616856
  168.8 8.3 %convolution_bitcast_fusion = f32[96]{0:T(128)S(1)} fusion(f32[96,27648]{1,0:T(8,128)S(1)} %fusion.19, f32[27648,1]{0,1:T(1,128)S(1)} %bitcast.89), kind=kOutput, calls=%fused_computation.45 | convolution fusion | flops 31850496 | bytes 10727808 | tf_op jit(solution)/shard_map/dot_general | solution.py:118
  177.1 14.5 %fusion.21 = f32[96,512]{1,0:T(8,128)S(1)} fusion(bf16[27648,512]{1,0:T(8,128)(2,1)} %param.9, f32[96,27648]{1,0:T(8,128)} %copy-done.2), kind=kOutput, calls=%fused_computation.35 | convolution fusion | flops 2720563200 | bytes 39124992 | tf_op jit(solution)/shard_map/dot_general | solution.py:117
  191.6 21.8 %all-reduce.5 = bf16[96,512]{1,0:T(8,128)(2,1)S(1)} all-reduce(f32[96,512]{1,0:T(8,128)S(1)} %fusion.21), channel_id=1, replica_groups=mesh['groups'=2,'vel'=4,'cell'=2,'sub'=2] {'vel'}, use_global_device_ids=true, to_apply=%region_3.4 | all-reduce | flops 49152 | bytes 294912 | tf_op jit(solution)/shard_map/psum | solution.py:119
  213.4 17.9 %convolution_multiply_fusion = f32[96,27648]{1,0:T(8,128)} fusion(bf16[27648,512]{1,0:T(8,128)(2,1)} %param.9, bf16[512,512]{1,0:T(8,128)(2,1)S(1)} %copy-done, bf16[96,512]{1,0:T(8,128)(2,1)S(1)} %all-reduce.5, f32[512]{0:T(512)S(1)} %copy-done.4), kind=kOutput, calls=%fused_computation | convolution fusion | flops 2770993152 | bytes 39553024 | tf_op jit(solution)/shard_map/dot_general | solution.py:121
  231.4 10.9 %fusion.83 = f32[5,96]{1,0:T(8,128)S(1)} fusion(f32[5,27648]{1,0:T(8,128)S(1)} %stack.14, f32[96,27648]{1,0:T(8,128)} %convolution_multiply_fusion), kind=kOutput, calls=%fused_computation.130 | convolution fusion | flops 159252480 | bytes 11171712 | tf_op jit(solution)/shard_map/dot_general | solution.py:124
  242.3 8.5 %all-reduce = (f32[96]{0:T(128)S(1)}, f32[5,96]{1,0:T(8,128)S(1)}) all-reduce(f32[96]{0:T(128)S(1)} %convolution_bitcast_fusion, f32[5,96]{1,0:T(8,128)S(1)} %fusion.83), channel_id=1, replica_groups=mesh['groups'=2,'vel'=4,'cell'=2,'sub'=2] {'vel'}, use_global_device_ids=true, to_apply=%region_5.6 | all-reduce | flops 576 | bytes 4608 | tf_op jit(solution)/shard_map/psum | solution.py:119
  250.8 14.1 %fusion.2 = bf16[96,27648]{1,0:T(8,128)(2,1)} fusion(f32[96,27648]{1,0:T(8,128)} %copy-done.2, f32[96,27648]{1,0:T(8,128)} %convolution_multiply_fusion, f32[5,96]{1,0:T(8,128)S(1)} %stack.37, f32[5,27648]{1,0:T(8,128)S(1)} %stack.14), kind=kOutput, calls=%fused_computation.6 | convolution fusion | flops 167215104 | bytes 27096960 | tf_op jit(solution)/shard_map/dot_general | solution.py:87
  (54 shorter events, 7.8 us)
Async XLA Ops:
  0.0 88.8 %copy-start = (bf16[512,512]{1,0:T(8,128)(2,1)S(1)}, bf16[512,512]{1,0:T(8,128)(2,1)}, u32[]{:S(2)}) copy-start(bf16[512,512]{1,0:T(8,128)(2,1)} %param.10) | copy-start | bytes 1572868
  0.0 14.9 %copy-start.5 = (s32[4]{0:T(128)S(1)}, s32[4]{0:T(128)}, u32[]{:S(2)}) copy-start(s32[4]{0:T(128)} %param.14) | copy-start | bytes 52
  0.0 17.9 %copy-start.3 = (f32[27648]{0:T(1024)S(1)}, f32[27648]{0:T(1024)}, u32[]{:S(2)}) copy-start(f32[27648]{0:T(1024)} %param.13) | copy-start | bytes 331780
  1.4 16.6 %collective-permute-start = (f32[2,27648]{1,0:T(2,128)S(1)}, f32[2,27648]{1,0:T(2,128)S(1)}, u32[]{:S(2)}, u32[]{:S(2)}) collective-permute-start(f32[2,27648]{1,0:T(2,128)S(1)} %get-tuple-element.21), channel_id=1, source_target_pairs={{0,1},{1,2},{2,3},{3,0},{4,5},{5,6},{6,7},{7,4},{8,9},{9,10},{10,1... | collective-permute-start | bytes 663560 | tf_op jit(solution)/shard_map/ppermute | solution.py:27
  1.9 16.1 %collective-permute-start.1 = (f32[2,27648]{1,0:T(2,128)S(1)}, f32[2,27648]{1,0:T(2,128)S(1)}, u32[]{:S(2)}, u32[]{:S(2)}) collective-permute-start(f32[2,27648]{1,0:T(2,128)S(1)} %get-tuple-element.22), channel_id=1, source_target_pairs={{1,0},{2,1},{3,2},{0,3},{5,4},{6,5},{7,6},{4,7},{9,8},{10,9},{11,1... | collective-permute-start | bytes 663560 | tf_op jit(solution)/shard_map/ppermute | solution.py:29
  18.1 18.2 %slice-start = ((s8[5308416]{0:T(1024)(128)(4,1)}), s8[4194304]{0:T(1024)(128)(4,1)S(1)}, s32[]{:S(2)}) async-start(s8[5308416]{0:T(1024)(128)(4,1)} %bitcast.86), calls=%async_computation | async-start | bytes 8388608
  18.2 18.2 %slice-start.1 = ((s8[5308416]{0:T(1024)(128)(4,1)}), s8[1114112]{0:T(1024)(128)(4,1)S(1)}, s32[]{:S(2)}) async-start(s8[5308416]{0:T(1024)(128)(4,1)} %bitcast.86), calls=%async_computation.1 | async-start | bytes 2228224
  38.1 4.1 %copy-start.1 = (f32[96,27648]{1,0:T(8,128)}, f32[96,27648]{1,0:T(8,128)S(1)}, u32[]{:S(2)}) copy-start(f32[96,27648]{1,0:T(8,128)S(1)} %fusion.20) | copy-start | bytes 31850500
  50.5 38.3 %copy-start.4 = (f32[512]{0:T(512)S(1)}, f32[512]{0:T(512)}, u32[]{:S(2)}) copy-start(f32[512]{0:T(512)} %param.11) | copy-start | bytes 6148
  106.7 19.5 %copy-start.6 = (f32[96]{0:T(128)S(1)}, f32[96]{0:T(128)}, u32[]{:S(2)}) copy-start(f32[96]{0:T(128)} %param.12) | copy-start | bytes 1156
  138.8 6.3 %collective-permute-start.2 = (f32[2,27648]{1,0:T(2,128)S(1)}, f32[2,27648]{1,0:T(2,128)S(1)}, u32[]{:S(2)}, u32[]{:S(2)}) collective-permute-start(f32[2,27648]{1,0:T(2,128)S(1)} %get-tuple-element.19), channel_id=1, source_target_pairs={{0,1},{1,2},{2,3},{3,0},{4,5},{5,6},{6,7},{7,4},{8,9},{9,10},{10,1... | collective-permute-start | bytes 663560 | tf_op jit(solution)/shard_map/ppermute | solution.py:27
  138.8 6.3 %collective-permute-start.3 = (f32[2,27648]{1,0:T(2,128)S(1)}, f32[2,27648]{1,0:T(2,128)S(1)}, u32[]{:S(2)}, u32[]{:S(2)}) collective-permute-start(f32[2,27648]{1,0:T(2,128)S(1)} %get-tuple-element.20), channel_id=1, source_target_pairs={{1,0},{2,1},{3,2},{0,3},{5,4},{6,5},{7,6},{4,7},{9,8},{10,9},{11,1... | collective-permute-start | bytes 663560 | tf_op jit(solution)/shard_map/ppermute | solution.py:29
  164.8 4.1 %copy-start.2 = (f32[96,27648]{1,0:T(8,128)}, f32[96,27648]{1,0:T(8,128)S(1)}, u32[]{:S(2)}) copy-start(f32[96,27648]{1,0:T(8,128)S(1)} %fusion.19) | copy-start | bytes 31850500
where the time goes:
time: 269 us; the launch traced here: 265 us
  matrix products  130 us (48%)
  blocking collectives  62.6 us (23%)
  other arithmetic  49.9 us (19%)
  local copies, waits for them, and re-layouts  12.2 us (5%)
  waiting for transfers between devices  4.61 us (2%)
  starting transfers between devices  4.29 us (2%)
    psum x4, blocking collectives, body(): encoded, energy_sum = lax.psum((partial_code, partial_energy), 'vel')  62.6 us
    dot_general x2, matrix products, body(): lax.dot_general(active, coder, (((1,), (1,)), ((), ())), preferred_elemen...  35.9 us
    mul x2, other arithmetic, advect(): flux = courant * jnp.where(courant >= 0.0, forward, backward)  29.3 us
    dot_general x2, matrix products, body(): partial_code = jnp.dot(coarse, coder, preferred_element_type=jnp.float32)  29 us
    dot_general x2, matrix products, project(): lax.dot_general(weights, basis, (((0,), (0,)), ((), ())), precision=lax.P...  26.4 us
    dot_general x2, matrix products, body(): lax.dot_general(basis, collision, (((1,), (1,)), ((), ())), precision=lax...  21.8 us
    dot_general x2, matrix products, body(): partial_energy = jnp.dot(fstar, basis[4], precision=lax.Precision.HIGHEST)  16.6 us
    sub x2, other arithmetic, advect(): return padded[2:length + 2] - (flux[1:] - flux[:-1])  9.98 us
  transfers between devices with their start and end apart: 4, of which 2 were waited for; matrix products, arithmetic and copies ran while one was open for 5% of the time, Pallas kernels for 0%

commit v1 on v0

v1 whole, which is shorter than its diff:
```python
import functools
import math

import jax
import jax.numpy as jnp
import numpy as np
from jax import lax
from jax.experimental import pallas as pl
from jax.experimental.pallas import tpu as pltpu
from jax.sharding import PartitionSpec as P

VGRID = 48
VBLOCKS = 96
VELS = 110592
WIDTH = VELS // VBLOCKS
SINK_RATE = 0.5
COURANT = 0.9
PACK = 4
EXT = 16
FIRST = 4
MESH = pl.DeviceIdType.MESH
BF16, F32 = jnp.bfloat16, jnp.float32


def grid_moments():
    centres = (2.0 * np.arange(VGRID) + 1.0 - VGRID) / VGRID
    second = float(np.sum(centres**2))
    fourth = float(np.sum(centres**4))
    number = float(VGRID)
    total = number**3
    cross = 3.0 * number * number * second
    quartic = 3.0 * number * number * fourth + 6.0 * number * second * second
    square = number * number * second
    return (total, cross, quartic, square)


def offsets(cells, count):
    rows = np.full(cells + EXT, 10**6)
    rows[:cells] = np.arange(cells)
    rows[cells : cells + 4] = [-2, -1, cells, cells + 1]
    second = rows[None, :] - rows[:cells, None]
    second = np.where(rows[None, :] > 10**5, 9, second)
    first = []
    for number in range(count):
        cols = np.full(cells + 2 * EXT, 10**7)
        cols[:cells] = np.arange(cells)
        at = cells + 4 * (number % PACK)
        cols[at : at + 4] = np.arange(-4, 0)
        cols[at + EXT : at + EXT + 4] = cells + np.arange(4)
        first.append(cols[None, :] - rows[:, None])
    first = np.stack(first)
    clean = lambda table: np.where(np.abs(table) <= 2, table, 9).astype(np.int32)
    return clean(first), clean(second)[None]


def stencil(courant, table):
    a = jnp.abs(courant)
    u = (1.0 - a) / 2.0
    q = (1.0 - a * a) / 6.0
    near = a * (1.0 - u + 3.0 * q)
    far = -a * q
    ahead = -a * (u - q)
    here = 1.0 - a * (1.0 - 2.0 * u + 3.0 * q)
    up = courant >= 0.0
    zero = jnp.zeros_like(a)
    weights = {
        -2: jnp.where(up, far, zero),
        -1: jnp.where(up, near, ahead),
        0: here,
        1: jnp.where(up, ahead, near),
        2: jnp.where(up, zero, far),
    }
    table = jnp.asarray(table)
    full = sum(jnp.where(table == o, w[:, None, None], 0.0) for o, w in weights.items())
    high = full.astype(BF16)
    low = (full - high.astype(F32)).astype(BF16)
    return jnp.concatenate([high, low], axis=2)


def dot(a, b):
    return jnp.dot(a, b, preferred_element_type=F32)


def dot_t(a, b, **kw):
    return lax.dot_general(a, b, (((1,), (1,)), ((), ())), preferred_element_type=F32, **kw)


def kernel(
    n, owners, cells, scale,
    coder_hbm, dens_hbm, left_ref, right_ref, basis_ref, a1_ref, a2_ref, energy_ref, inflow_ref,
    keep_ref, w_ref, bias_ref, rest_ref,
    out_hbm,
    coder_v, p_v, f_v, acc, eacc, send, recv, part, gath, esend, erecv, bsend, brecv, bgath, mult, act_v,
    coder_sem, dens_sem, out_sem, s_send, s_recv, g_send, g_recv, e_send, e_recv, b_send, b_recv, c_send, c_recv,
):
    me = lax.axis_index("vel")
    count = coder_v.shape[0]
    rows = cells + EXT
    latent = coder_v.shape[2]
    piece = latent // owners

    def coder_copy(b):
        return pltpu.make_async_copy(coder_hbm.at[b], coder_v.at[b], coder_sem.at[b])

    def columns(b):
        return pl.ds(pl.multiple_of(b * WIDTH, 128), WIDTH)

    def dens_copy(b):
        return pltpu.make_async_copy(dens_hbm.at[:, columns(b)], p_v.at[b], dens_sem.at[b])

    def out_copy(b):
        return pltpu.make_async_copy(p_v.at[b], out_hbm.at[:, columns(b)], out_sem.at[b])

    @pl.loop(0, count)
    def _(b):
        dens_copy(b).start()
        coder_copy(b).start()

    barrier = pltpu.get_barrier_semaphore()
    for d in range(1, n):
        pl.semaphore_signal(
            barrier, inc=1, device_id={"vel": lax.rem(me + d, n)}, device_id_type=MESH
        )
    pl.semaphore_wait(barrier, n - 1)

    def only(test, run):
        if n == owners:
            run()
        else:
            pl.when(test)(run)

    def energy_of(f, b):
        e = energy_ref[b]
        total = f[:, :128] * e[:, :128]
        for g in range(128, WIDTH, 128):
            total += f[:, g : g + 128] * e[:, g : g + 128]
        return total

    def exchange(step, size):
        col = jnp.sum(eacc[:size], axis=1, keepdims=True)
        eye = lax.broadcasted_iota(jnp.int32, (size, 128), 0) == lax.broadcasted_iota(
            jnp.int32, (size, 128), 1
        )
        row = jnp.sum(jnp.where(eye, col, 0.0), axis=0, keepdims=True)
        esend[step] = jnp.broadcast_to(row, (8, 128))
        for q in range(owners):
            value = acc[:size, q * piece : (q + 1) * piece]
            part[q, :size] = value
            send[step, q, :size] = value.astype(BF16)
            if step == 0:
                bsend[q] = acc[cells:rows, q * piece : (q + 1) * piece]

        def remote(src, dst, ss, rs, d):
            return pltpu.make_async_remote_copy(
                src_ref=src, dst_ref=dst, send_sem=ss, recv_sem=rs,
                device_id={"vel": lax.rem(me + d, n)}, device_id_type=MESH,
            )

        def scatter(d):
            to = lax.rem(me + d, n)
            made = [
                remote(
                    send.at[step, to, pl.ds(0, size)], recv.at[step, d - 1, pl.ds(0, size)],
                    s_send.at[step, d - 1], s_recv.at[step, d - 1], d,
                )
            ]
            if step == 0:
                made.append(
                    remote(bsend.at[to], brecv.at[d - 1], b_send.at[d - 1], b_recv.at[d - 1], d)
                )
            return made

        def spread(d):
            made = [
                remote(
                    gath.at[step, me, pl.ds(0, size)], gath.at[step, me, pl.ds(0, size)],
                    g_send.at[step, d - 1], g_recv.at[step, me], d,
                )
            ]
            if step == 0:
                made.append(
                    remote(bgath.at[me], bgath.at[me], c_send.at[d - 1], c_recv.at[me], d)
                )
            return made

        def arrival(owner):
            made = [
                remote(
                    gath.at[step, owner, pl.ds(0, size)], gath.at[step, owner, pl.ds(0, size)],
                    g_send.at[step, 0], g_recv.at[step, owner], 1,
                )
            ]
            if step == 0:
                made.append(
                    remote(bgath.at[owner], bgath.at[owner], c_send.at[0], c_recv.at[owner], 1)
                )
            return made

        def tell(d):
            return remote(
                esend.at[step], erecv.at[step, d - 1], e_send.at[step, d - 1], e_recv.at[step, d - 1], d
            )

        for d in range(1, n):
            only(lax.rem(me + d, n) < owners, lambda d=d: [c.start() for c in scatter(d)] and None)
        for d in range(1, n):
            tell(d).start()

        def reduce():
            total = part[me, :size]
            for d in range(1, n):
                for c in scatter(d):
                    c.wait_recv()
                total += recv[step, d - 1, :size].astype(F32)
            gath[step, me, :size] = total.astype(BF16)
            if step == 0:
                base = bsend[me]
                for d in range(1, n):
                    base += brecv[d - 1]
                bgath[me] = base
            for d in range(1, n):
                for c in spread(d):
                    c.start()

        only(me < owners, reduce)
        for d in range(1, n):
            only(lax.rem(me + d, n) < owners, lambda d=d: [c.wait_send() for c in scatter(d)] and None)
        for d in range(1, n):
            tell(d).wait()
        only(me < owners, lambda: [c.wait_send() for d in range(1, n) for c in spread(d)] and None)
        for d in range(1, n):
            owner = lax.rem(me + d, n)
            only(owner < owners, lambda owner=owner: [c.wait_recv() for c in arrival(owner)] and None)
        row = esend[step]
        for d in range(1, n):
            row += erecv[step, d - 1]
        return jnp.sum(jnp.where(eye, row[:1], 0.0), axis=1, keepdims=True)

    def latent_layer(step, size):
        energy_sum = exchange(step, size)
        encoded = jnp.concatenate([gath[step, q, :size] for q in range(owners)], axis=1)
        active = jnp.tanh(dot(encoded, w_ref[...]) + bias_ref[...]).astype(BF16)
        act_v[:size] = active
        base = jnp.concatenate([bgath[q] for q in range(owners)], axis=1)
        sums = scale * dot_t(active.astype(F32), base, precision=lax.Precision.HIGHEST)
        total, cross, quartic, square = grid_moments()
        sink = -SINK_RATE * (1.0 - rest_ref[:size] * rest_ref[:size]) * energy_sum
        grid = float(VGRID)
        m = [sums[:, FIRST + i : FIRST + i + 1] for i in range(6)]
        excess = (m[4] + m[5]) / (grid * grid) - sink
        determinant = total * quartic - cross * cross
        mass_mult = (quartic * m[0] - cross * excess) / determinant
        energy_mult = (total * excess - cross * m[0]) / determinant / (grid * grid)
        values = [mass_mult] + [m[i] / (square * grid * grid) for i in (1, 2, 3)] + [energy_mult] * 2
        lane = lax.broadcasted_iota(jnp.int32, (size, 2 * EXT), 1)
        full = jnp.zeros((size, 2 * EXT), F32)
        for i, value in enumerate(values):
            full = jnp.where(lane % EXT == FIRST + i, -value, full)
        high = full.astype(BF16).astype(F32)
        mult[:size] = jnp.where(lane < EXT, high, full - high).astype(BF16)

    def advanced(b, size):
        base = basis_ref[b]
        collision = dot_t(act_v[:size], coder_v[b])
        correction = dot(mult[:size], jnp.concatenate([base, base], axis=0))
        return (f_v[b, :size] + correction + scale * collision).astype(BF16)

    acc[...] = jnp.zeros_like(acc)
    eacc[...] = jnp.zeros_like(eacc)
    extra = lax.broadcasted_iota(jnp.int32, (EXT, WIDTH), 0) >= FIRST

    @pl.loop(0, count)
    def _(b):
        dens_copy(b).wait()
        x = jnp.concatenate([p_v[b], left_ref[b // PACK], right_ref[b // PACK]], axis=0)
        f = dot(a1_ref[b], jnp.concatenate([x, x], axis=0))
        f_v[b] = f
        eacc[...] += energy_of(f, b)
        coarse = f.astype(BF16)
        tail = jnp.where(extra, basis_ref[b].astype(F32), f[cells:]).astype(BF16)
        coder_copy(b).wait()
        acc[...] += dot(jnp.concatenate([coarse[:cells], tail], axis=0), coder_v[b])

    latent_layer(0, rows)
    acc[...] = jnp.zeros_like(acc)
    eacc[...] = jnp.zeros_like(eacc)

    @pl.loop(0, count)
    def _(b):
        state = advanced(b, rows)
        edge = jnp.where(keep_ref[...] > 0.0, state[cells:].astype(F32), inflow_ref[b]).astype(BF16)
        x = jnp.concatenate([state[:cells], edge], axis=0)
        f = dot(a2_ref[b], jnp.concatenate([x, x], axis=0))
        f_v[b, :cells] = f
        eacc[:cells] += energy_of(f, b)
        acc[:cells] += dot(f.astype(BF16), coder_v[b])

    latent_layer(1, cells)

    @pl.loop(0, count)
    def _(b):
        p_v[b] = advanced(b, cells)
        out_copy(b).start()

    @pl.loop(0, count)
    def _(b):
        out_copy(b).wait()


def ring(value, step):
    count = lax.axis_size("cell") * lax.axis_size("sub")
    return lax.ppermute(value, ("cell", "sub"), [(i, (i + step) % count) for i in range(count)])


def body(density, coder, w_latent, b_latent, restitution, inflow, flags, blocks):
    cells, columns = density.shape
    latent = coder.shape[1]
    count = columns // WIDTH
    chunks = -(-count // PACK)
    n = lax.axis_size("vel")
    owners = min(n, latent // 128)
    rows = cells + EXT

    left = ring(density[-4:], 1)
    right = ring(density[:4], -1)
    rest_left = ring(restitution[-2:], 1)
    rest_right = ring(restitution[:2], -1)

    sub_count = lax.axis_size("sub")
    position = lax.axis_index("cell") * sub_count + lax.axis_index("sub")
    block_count = lax.axis_size("cell") * sub_count
    open_left = lax.dynamic_index_in_dim(flags, position, 0, keepdims=False) == 1
    open_right = (
        lax.dynamic_index_in_dim(flags, (position + 1) % block_count, 0, keepdims=False) == 1
    )

    number = blocks[:, None] * WIDTH + jnp.arange(WIDTH, dtype=jnp.int32)[None, :]
    nx = 2 * (number // (VGRID * VGRID)) + 1 - VGRID
    ny = 2 * (number // VGRID % VGRID) + 1 - VGRID
    nz = 2 * (number % VGRID) + 1 - VGRID
    kinetic = nx * nx + ny * ny + nz * nz
    upper = kinetic // 64 * 64
    zero = jnp.zeros_like(nx)
    basis = jnp.stack(
        [zero] * FIRST + [zero + 1, nx, ny, nz, upper, kinetic - upper] + [zero] * (EXT - FIRST - 6),
        axis=1,
    ).astype(BF16)
    energy = (kinetic.astype(F32) / (VGRID * VGRID))[:, None, :]
    along = 2 * (blocks * WIDTH // (VGRID * VGRID)) + 1 - VGRID
    courant = COURANT * (along.astype(F32) / VGRID)
    first, second = offsets(cells, count)
    a1 = stencil(courant, first)
    a2 = stencil(courant, second)

    def packed(ghosts, is_open):
        ghosts = jnp.where(is_open, ghosts, inflow.astype(BF16)[None])
        ghosts = ghosts.reshape(4, count, WIDTH).transpose(1, 0, 2)
        ghosts = jnp.pad(ghosts, ((0, chunks * PACK - count), (0, 0), (0, 0)))
        return ghosts.reshape(chunks, PACK * 4, WIDTH)

    rest = jnp.concatenate([restitution, rest_left, rest_right, jnp.zeros((EXT - 4,), F32)])
    side = jnp.arange(EXT)
    keep = jnp.where(side < 2, open_left, jnp.where(side < 4, open_right, True)).astype(F32)

    vmem = pl.BlockSpec(memory_space=pltpu.VMEM)
    hbm = pl.BlockSpec(memory_space=pl.ANY)
    dma = pltpu.SemaphoreType.DMA
    piece = latent // owners
    others = max(n - 1, 1)
    flops = 2 * columns * latent * (4 * rows) + 2 * columns * 512 * rows
    return pl.pallas_call(
        functools.partial(kernel, n, owners, cells, math.sqrt(VELS / latent)),
        out_shape=jax.ShapeDtypeStruct((cells, columns), BF16),
        in_specs=[hbm, hbm] + [vmem] * 11,
        out_specs=hbm,
        scratch_shapes=[
            pltpu.VMEM((count, WIDTH, latent), BF16),
            pltpu.VMEM((count, cells, WIDTH), BF16),
            pltpu.VMEM((count, rows, WIDTH), F32),
            pltpu.VMEM((rows, latent), F32),
            pltpu.VMEM((rows, 128), F32),
            pltpu.VMEM((2, owners, rows, piece), BF16),
            pltpu.VMEM((2, others, rows, piece), BF16),
            pltpu.VMEM((owners, rows, piece), F32),
            pltpu.VMEM((2, owners, rows, piece), BF16),
            pltpu.VMEM((2, 8, 128), F32),
            pltpu.VMEM((2, others, 8, 128), F32),
            pltpu.VMEM((owners, EXT, piece), F32),
            pltpu.VMEM((others, EXT, piece), F32),
            pltpu.VMEM((owners, EXT, piece), F32),
            pltpu.VMEM((rows, 2 * EXT), BF16),
            pltpu.VMEM((rows, latent), BF16),
            dma((count,)), dma((count,)), dma((count,)),
            dma((2, others)), dma((2, others)), dma((2, others)), dma((2, owners)),
            dma((2, others)), dma((2, others)),
            dma((others,)), dma((others,)), dma((others,)), dma((owners,)),
        ],
        compiler_params=pltpu.CompilerParams(
            collective_id=0, has_side_effects=True, vmem_limit_bytes=60 * 1024 * 1024
        ),
        cost_estimate=pl.CostEstimate(
            flops=flops, bytes_accessed=2 * columns * (latent + 2 * cells), transcendentals=0
        ),
    )(
        coder.reshape(count, WIDTH, latent), density,
        packed(left, open_left), packed(right, open_right), basis, a1, a2, energy,
        inflow.reshape(count, 1, WIDTH), keep[:, None], w_latent, b_latent[None, :], rest[:, None],
    )


def solution(mesh):
    return jax.shard_map(
        body,
        mesh=mesh,
        in_specs=(
            P(("groups", "cell", "sub"), "vel"),
            P("vel", None),
            P(),
            P(),
            P(("groups", "cell", "sub")),
            P(("groups", "vel")),
            P("groups"),
            P(("groups", "vel")),
        ),
        out_specs=P(("groups", "cell", "sub"), "vel"),
        check_vma=False,
    )
```

time: 269 us -> 112 us (0.42); the launches traced: 265 us -> 111 us
  matrix products: 130 us -> 0 us
  Pallas kernels: 0 us -> 79.4 us
  blocking collectives: 62.6 us -> 0 us
  other arithmetic: 49.9 us -> 13.1 us
  waiting for transfers between devices: 4.61 us -> 0.01 us
    dot_general x10 -> x0, matrix products: 130 us -> none  [the longest x2 35.9 us: body(): lax.dot_general(active, coder, (((1,), (1,)), ((), ())), preferred_elemen...]
    pallas_call x0 -> x1, Pallas kernels: none -> 79.4 us  [body(): pl.pallas_call(functools.partial(kernel, n, owners, cells, math.sqrt(VELS...]
    psum x4 -> x0, blocking collectives: 62.6 us -> none  [body(): encoded, energy_sum = lax.psum((partial_code, partial_energy), 'vel')]
    mul x3 -> x1, other arithmetic: 30 us -> 0.66 us  [body(): blocks[:, None] * WIDTH + jnp.arange(WIDTH, dtype=jnp.int32)[None, :]]
    sub x2 -> x0, other arithmetic: 9.98 us -> none  [advect(): return padded[2:length + 2] - (flux[1:] - flux[:-1])]
    convert_element_type x1 -> x4, other arithmetic: 7.47 us -> 2.56 us  [the longest x1 1.17 us: stencil(): low = (full - high.astype(F32)).astype(BF16)]
    ppermute x4, waiting for transfers between devices: 4.61 us -> 0.01 us  [ring(): lax.ppermute(value, ('cell', 'sub'), [(i, (i + step) % count) for i in ra...]
    unnamed x23 -> x27, local copies, waits for them, and re-layouts: 8.68 us -> 5.29 us
  transfers between devices with their start and end apart: 4 -> 4, of which waited for: 2 -> 0; matrix products, arithmetic and copies ran while one was open for 5% -> 18% of each run, Pallas kernels for 0% -> 0%
where the time goes in v1:
time: 112 us; the launch traced here: 111 us
  Pallas kernels  79.4 us (71%)
  local copies, waits for them, and re-layouts  14.2 us (13%)
  other arithmetic  13.1 us (12%)
  starting transfers between devices  3.17 us (3%)
  between operations  1.46 us (1%)
    pallas_call x1, Pallas kernels, body(): pl.pallas_call(functools.partial(kernel, n, owners, cells, math.sqrt(VELS...  79.4 us
    unnamed x27, local copies, waits for them, and re-layouts  5.29 us
    another operation x3, local copies, waits for them, and re-layouts, body(): jnp.stack([zero] * FIRST + [zero + 1, nx, ny, nz, upper, kinetic - upper]...  3.93 us
    ppermute x4, starting transfers between devices, ring(): lax.ppermute(value, ('cell', 'sub'), [(i, (i + step) % count) for i in ra...  3.17 us
    another operation x1, other arithmetic  3.13 us
    div x1, other arithmetic, body(): energy = (kinetic.astype(F32) / (VGRID * VGRID))[:, None, :]  2.97 us
    concatenate x2, other arithmetic, stencil(): return jnp.concatenate([high, low], axis=2)  2.82 us
  transfers between devices with their start and end apart: 4, of which 0 were waited for; matrix products, arithmetic and copies ran while one was open for 18% of the time, Pallas kernels for 0%

profile of v1, /device:TPU:0, one launch (start us, length us, event | category | flops | bytes accessed | tf_op | source)
XLA Modules:
  0.0 111.4 jit_solution(15390181740281289224)
XLA Ops:
  0.0 0.8 fusion.20
  0.9 0.5 collective-permute-start.2
  1.3 1.9 %collective-permute-start.3 = (f32[2]{0:T(128)S(1)}, f32[2]{0:T(128)S(1)}, u32[]{:S(2)}, u32[]{:S(2)}) collective-permute-start(f32[2]{0:T(128)S(1)} %get-tuple-element.16), channel_id=1, source_target_pairs={{0,3},{1,0},{2,1},{3,2},{4,7},{5,4},{6,5},{7,6},{8,11},{9,8},{10,9... | collective-permute-start | bytes 32 | tf_op jit(solution)/shard_map/ppermute | solution.py:312
  3.3 1.3 %fusion.19 = (bf16[4,27648]{1,0:T(4,128)(2,1)S(1)}, bf16[4,27648]{1,0:T(4,128)(2,1)S(1)}) fusion(bf16[96,27648]{1,0:T(8,128)(2,1)} %dens_hbm.1), kind=kLoop, calls=%fused_computation.53 | loop fusion | bytes 884736 | tf_op jit(solution)/shard_map/slice | solution.py:325
  4.6 0.7 collective-permute-start.1
  5.3 0.1 collective-permute-start
  5.4 0.7 broadcast_multiply_fusion
  6.0 0.7 broadcast_select_fusion.3
  6.7 3.0 %convert_multiply_fusion.energy_ref = f32[24,1,1152]{2,1,0:T(1,128)} fusion(s32[24]{0:T(128)S(1)} %broadcast_multiply_fusion), kind=kLoop, calls=%fused_computation.22 | loop fusion | flops 1050624 | bytes 110688 | tf_op jit(solution)/shard_map/div | solution.py:348
  9.7 3.1 %subtract_convert_fusion.2 = (bf16[24,1,1152]{2,1,0:T(2,128)(2,1)S(1)}, bf16[24,1,1152]{2,1,0:T(2,128)(2,1)S(1)}, bf16[24,1,1152]{2,1,0:T(2,128)(2,1)S(1)}, bf16...) fusion(s32[24]{0:T(128)S(1)} %broadcast_multiply_fusion), kind=kLoop, calls=%fused_computation.23 | loop fusion | flops 1603584 | bytes 276576 | tf_op jit(solution)/shard_map/convert.6
  12.8 0.6 fusion.21
  14.7 0.8 fusion.1
  15.6 1.6 %pad_maximum_fusion.1.a2_ref = bf16[24,96,224]{2,1,0:T(8,128)(2,1)} fusion(bf16[24,96,112]{2,1,0:T(8,128)(2,1)S(1)} %get-tuple-element.12, bf16[24,96,112]{2,1,0:T(8,128)(2,1)S(1)} %get-tuple-element.11), kind=kLoop, calls=%fused_computation.4 | loop fusion | flops 2064384 | bytes 2064384 | tf_op jit(solution)/shard_map/concatenate | solution.py:77
  17.2 1.2 %subtract_convert_fusion = (bf16[24,112,128]{2,1,0:T(8,128)(2,1)S(1)}, bf16[24,112,128]{2,1,0:T(8,128)(2,1)S(1)}) fusion(pred[24,112,128]{2,1,0:T(8,128)(4,1)S(1)} %copy-done, pred[24,112,128]{2,1,0:T(8,128)(4,1)S(1)} %copy-done.1, pred[24,112,128]{2,1,0:T(8,128)(4,1)S(1)} %copy-done.2, pred[24,112,128]{2,1,0:T(8,128)(4,1)S(1)} %copy-done.3, ...), kind=kLoop, calls=%fused_computation.1 | loop fusion | flops 4472832 | bytes 3097056 | tf_op jit(solution)/shard_map/convert_element_type | solution.py:76
  18.4 1.2 %pad_maximum_fusion.a1_ref = bf16[24,112,256]{2,1,0:T(8,128)(2,1)} fusion(bf16[24,112,128]{2,1,0:T(8,128)(2,1)S(1)} %get-tuple-element.5, bf16[24,112,128]{2,1,0:T(8,128)(2,1)S(1)} %get-tuple-element.6), kind=kLoop, calls=%fused_computation | loop fusion | flops 2752512 | bytes 2752512 | tf_op jit(solution)/shard_map/concatenate | solution.py:77
  19.8 3.8 %stack.20.basis_ref = bf16[24,16,1152]{2,1,0:T(8,128)(2,1)} concatenate(bf16[24,4,1152]{2,1,0:T(4,128)(2,1)S(1)} %broadcast.733, bf16[24,1,1152]{2,1,0:T(2,128)(2,1)S(1)} %stack.17, bf16[24,1,1152]{2,1,0:T(2,128)(2,1)S(1)} %get-tuple-element.23, bf16[24,1,1152]{2,1,0:T(2,128)(2,1)S(1)} %get-tuple-element.25, bf16[24,1,1152]{2,1,0:T(2,128)(2,1)S(1)} %get-tuple-element.22, ...), dimensions={1} | concatenate | bytes 1769472 | tf_op jit(solution)/shard_map/stack | solution.py:344
  23.6 0.6 fusion.14.keep_ref
  24.2 0.1 maximum_bitcast_fusion
  24.3 0.7 copy.13.rest_ref
  25.1 0.2 broadcast_select_fusion
  25.3 0.7 reshape.339.right_ref
  26.0 0.7 reshape.337.left_ref
  26.8 79.4 %shard_map.100 = bf16[96,27648]{1,0:T(8,128)(2,1)} custom-call(bf16[24,1152,512]{2,1,0:T(8,128)(2,1)} %bitcast.26, bf16[96,27648]{1,0:T(8,128)(2,1)} %dens_hbm.1, bf16[6,16,1152]{2,1,0:T(8,128)(2,1)} %reshape.337.left_ref, bf16[6,16,1152]{2,1,0:T(8,128)(2,1)} %reshape.339.right_ref, bf16[24,16,1152]{2,1,0:T(8,128)(2,1)} %stack.20.basis_ref, ...), custom_call_target="tpu_custom_call" | custom-call | flops 15854469120 | bytes 38928384 | tf_op jit(solution)/shard_map/pallas_call | solution.py:371
  106.2 5.2 %copy.15 = bf16[96,27648]{1,0:T(8,128)(2,1)} copy(bf16[96,27648]{1,0:T(8,128)(2,1)} %shard_map.100) | data formatting | bytes 10616832
  (36 shorter events, 0.3 us)
Async XLA Ops:
  0.0 14.7 %copy-start.6 = (pred[96,112]{1,0:T(32,128)(4,1)S(1)}, pred[96,112]{1,0:T(32,128)(4,1)}, u32[]{:S(2)}) copy-start(pred[96,112]{1,0:T(32,128)(4,1)} %constant.161) | copy-start | bytes 32260
  0.0 14.7 %copy-start.7 = (pred[96,112]{1,0:T(32,128)(4,1)S(1)}, pred[96,112]{1,0:T(32,128)(4,1)}, u32[]{:S(2)}) copy-start(pred[96,112]{1,0:T(32,128)(4,1)} %constant.159) | copy-start | bytes 32260
  0.0 14.7 %copy-start.8 = (pred[96,112]{1,0:T(32,128)(4,1)S(1)}, pred[96,112]{1,0:T(32,128)(4,1)}, u32[]{:S(2)}) copy-start(pred[96,112]{1,0:T(32,128)(4,1)} %constant.157) | copy-start | bytes 32260
  0.0 14.7 %copy-start.9 = (pred[96,112]{1,0:T(32,128)(4,1)S(1)}, pred[96,112]{1,0:T(32,128)(4,1)}, u32[]{:S(2)}) copy-start(pred[96,112]{1,0:T(32,128)(4,1)} %constant.155) | copy-start | bytes 32260
  0.0 14.7 %copy-start.10 = (pred[96,112]{1,0:T(32,128)(4,1)S(1)}, pred[96,112]{1,0:T(32,128)(4,1)}, u32[]{:S(2)}) copy-start(pred[96,112]{1,0:T(32,128)(4,1)} %constant.153) | copy-start | bytes 32260
  0.0 12.8 %copy-start.12 = (s32[4]{0:T(128)S(1)}, s32[4]{0:T(128)}, u32[]{:S(2)}) copy-start(s32[4]{0:T(128)} %param.16) | copy-start | bytes 52
  0.0 14.6 %copy-start.5 = (f32[27648]{0:T(1024)S(1)}, f32[27648]{0:T(1024)}, u32[]{:S(2)}) copy-start(f32[27648]{0:T(1024)} %param.15) | copy-start | bytes 331780
  0.9 23.4 %collective-permute-start.2 = (f32[2]{0:T(128)S(1)}, f32[2]{0:T(128)S(1)}, u32[]{:S(2)}, u32[]{:S(2)}) collective-permute-start(f32[2]{0:T(128)S(1)} %get-tuple-element.15), channel_id=1, source_target_pairs={{0,1},{1,2},{2,3},{3,0},{4,5},{5,6},{6,7},{7,4},{8,9},{9,10},{10,1... | collective-permute-start | bytes 32 | tf_op jit(solution)/shard_map/ppermute | solution.py:312
  1.3 22.9 %collective-permute-start.3 = (f32[2]{0:T(128)S(1)}, f32[2]{0:T(128)S(1)}, u32[]{:S(2)}, u32[]{:S(2)}) collective-permute-start(f32[2]{0:T(128)S(1)} %get-tuple-element.16), channel_id=1, source_target_pairs={{0,3},{1,0},{2,1},{3,2},{4,7},{5,4},{6,5},{7,6},{8,11},{9,8},{10,9... | collective-permute-start | bytes 32 | tf_op jit(solution)/shard_map/ppermute | solution.py:312
  4.6 20.5 %collective-permute-start.1 = (bf16[4,27648]{1,0:T(4,128)(2,1)S(1)}, bf16[4,27648]{1,0:T(4,128)(2,1)S(1)}, u32[]{:S(2)}, u32[]{:S(2)}) collective-permute-start(bf16[4,27648]{1,0:T(4,128)(2,1)S(1)} %get-tuple-element.9), channel_id=1, source_target_pairs={{0,3},{1,0},{2,1},{3,2},{4,7},{5,4},{6,5},{7,6},{8,11},{9,8},{10,9... | collective-permute-start | bytes 663560 | tf_op jit(solution)/shard_map/ppermute | solution.py:312
  5.3 19.8 %collective-permute-start = (bf16[4,27648]{1,0:T(4,128)(2,1)S(1)}, bf16[4,27648]{1,0:T(4,128)(2,1)S(1)}, u32[]{:S(2)}, u32[]{:S(2)}) collective-permute-start(bf16[4,27648]{1,0:T(4,128)(2,1)S(1)} %get-tuple-element.10), channel_id=1, source_target_pairs={{0,1},{1,2},{2,3},{3,0},{4,5},{5,6},{6,7},{7,4},{8,9},{9,10},{10,1... | collective-permute-start | bytes 663560 | tf_op jit(solution)/shard_map/ppermute | solution.py:312
  15.5 1.7 %copy-start = (pred[24,112,128]{2,1,0:T(8,128)(4,1)S(1)}, pred[24,112,128]{2,1,0:T(8,128)(4,1)}, u32[]{:S(2)}) copy-start(pred[24,112,128]{2,1,0:T(8,128)(4,1)} %constant.151) | copy-start | bytes 1032196
  15.5 1.6 %copy-start.1 = (pred[24,112,128]{2,1,0:T(8,128)(4,1)S(1)}, pred[24,112,128]{2,1,0:T(8,128)(4,1)}, u32[]{:S(2)}) copy-start(pred[24,112,128]{2,1,0:T(8,128)(4,1)} %constant.150) | copy-start | bytes 1032196
  15.6 1.6 %copy-start.2 = (pred[24,112,128]{2,1,0:T(8,128)(4,1)S(1)}, pred[24,112,128]{2,1,0:T(8,128)(4,1)}, u32[]{:S(2)}) copy-start(pred[24,112,128]{2,1,0:T(8,128)(4,1)} %constant.149) | copy-start | bytes 1032196
  15.6 1.6 %copy-start.3 = (pred[24,112,128]{2,1,0:T(8,128)(4,1)S(1)}, pred[24,112,128]{2,1,0:T(8,128)(4,1)}, u32[]{:S(2)}) copy-start(pred[24,112,128]{2,1,0:T(8,128)(4,1)} %constant.148) | copy-start | bytes 1032196
  15.6 1.6 %copy-start.4 = (pred[24,112,128]{2,1,0:T(8,128)(4,1)S(1)}, pred[24,112,128]{2,1,0:T(8,128)(4,1)}, u32[]{:S(2)}) copy-start(pred[24,112,128]{2,1,0:T(8,128)(4,1)} %constant.147) | copy-start | bytes 1032196
  19.6 4.6 %copy-start.11 = (f32[96]{0:T(128)S(1)}, f32[96]{0:T(128)}, u32[]{:S(2)}) copy-start(f32[96]{0:T(128)} %param.14) | copy-start | bytes 1156

commit v2 on v1

--- a/solution.py
+++ b/solution.py
@@ -34,47 +34,52 @@
     return (total, cross, quartic, square)
 
 
-def offsets(cells, count):
+def tables(cells):
     rows = np.full(cells + EXT, 10**6)
     rows[:cells] = np.arange(cells)
     rows[cells : cells + 4] = [-2, -1, cells, cells + 1]
     second = rows[None, :] - rows[:cells, None]
     second = np.where(rows[None, :] > 10**5, 9, second)
-    first = []
-    for number in range(count):
-        cols = np.full(cells + 2 * EXT, 10**7)
-        cols[:cells] = np.arange(cells)
-        at = cells + 4 * (number % PACK)
-        cols[at : at + 4] = np.arange(-4, 0)
-        cols[at + EXT : at + EXT + 4] = cells + np.arange(4)
-        first.append(cols[None, :] - rows[:, None])
-    first = np.stack(first)
-    clean = lambda table: np.where(np.abs(table) <= 2, table, 9).astype(np.int32)
-    return clean(first), clean(second)[None]
+    cols = np.arange(cells + 2 * EXT)
+    cols[cells : cells + EXT] = np.arange(EXT) % 4 - 4
+    cols[cells + EXT :] = cells + np.arange(EXT) % 4
+    first = cols[None, :] - rows[:, None]
+    group = np.full((8, cells + 2 * EXT), -1)
+    group[:, cells:] = np.arange(2 * EXT) % EXT // 4
+    clean = lambda table: np.where(np.abs(table) <= 2, table, 9)
+    return [t.astype(np.float32) for t in (clean(first), clean(second), group)]
+
+
+def fixed_rows():
+    column = np.arange(WIDTH)
+    rows = np.zeros((8, WIDTH), np.float32)
+    rows[0] = 2 * (column // VGRID % VGRID) + 1 - VGRID
+    rows[1] = 2 * (column % VGRID) + 1 - VGRID
+    return rows
 
 
 def stencil(courant, table):
     a = jnp.abs(courant)
-    u = (1.0 - a) / 2.0
-    q = (1.0 - a * a) / 6.0
+    u = (1.0 - a) * 0.5
+    q = (1.0 - a * a) * (1.0 / 6.0)
     near = a * (1.0 - u + 3.0 * q)
     far = -a * q
     ahead = -a * (u - q)
     here = 1.0 - a * (1.0 - 2.0 * u + 3.0 * q)
     up = courant >= 0.0
-    zero = jnp.zeros_like(a)
     weights = {
-        -2: jnp.where(up, far, zero),
+        -2: jnp.where(up, far, 0.0),
         -1: jnp.where(up, near, ahead),
         0: here,
         1: jnp.where(up, ahead, near),
-        2: jnp.where(up, zero, far),
+        2: jnp.where(up, 0.0, far),
     }
-    table = jnp.asarray(table)
-    full = sum(jnp.where(table == o, w[:, None, None], 0.0) for o, w in weights.items())
+    full = jnp.zeros(table.shape, F32)
+    for offset, weight in weights.items():
+        full = jnp.where(table == offset, weight, full)
     high = full.astype(BF16)
     low = (full - high.astype(F32)).astype(BF16)
-    return jnp.concatenate([high, low], axis=2)
+    return jnp.concatenate([high, low], axis=1)
 
 
 def dot(a, b):
@@ -87,11 +92,11 @@
 
 def kernel(
     n, owners, cells, scale,
-    coder_hbm, dens_hbm, left_ref, right_ref, basis_ref, a1_ref, a2_ref, energy_ref, inflow_ref,
-    keep_ref, w_ref, bias_ref, rest_ref,
+    blocks_ref, coder_hbm, dens_hbm, left_ref, right_ref, first_ref, second_ref, group_ref, fixed_ref,
+    inflow_ref, keep_ref, w_ref, bias_ref, rest_ref,
     out_hbm,
-    coder_v, p_v, f_v, acc, eacc, send, recv, part, gath, esend, erecv, bsend, brecv, bgath, mult, act_v,
-    coder_sem, dens_sem, out_sem, s_send, s_recv, g_send, g_recv, e_send, e_recv, b_send, b_recv, c_send, c_recv,
+    basis_ref, energy_ref, coder_v, p_v, f_v, acc, eacc, send, recv, part, precv, gath, esend, erecv, bgath, mult, act_v,
+    coder_sem, dens_sem, out_sem, s_send, s_recv, g_send, g_recv, e_send, e_recv, c_send, c_recv,
 ):
     me = lax.axis_index("vel")
     count = coder_v.shape[0]
@@ -146,9 +151,8 @@
         for q in range(owners):
             value = acc[:size, q * piece : (q + 1) * piece]
             part[q, :size] = value
-            send[step, q, :size] = value.astype(BF16)
-            if step == 0:
-                bsend[q] = acc[cells:rows, q * piece : (q + 1) * piece]
+            if step:
+                send[q, :size] = value.astype(BF16)
 
         def remote(src, dst, ss, rs, d):
             return pltpu.make_async_remote_copy(
@@ -158,17 +162,11 @@
 
         def scatter(d):
             to = lax.rem(me + d, n)
-            made = [
-                remote(
-                    send.at[step, to, pl.ds(0, size)], recv.at[step, d - 1, pl.ds(0, size)],
-                    s_send.at[step, d - 1], s_recv.at[step, d - 1], d,
-                )
-            ]
             if step == 0:
-                made.append(
-                    remote(bsend.at[to], brecv.at[d - 1], b_send.at[d - 1], b_recv.at[d - 1], d)
-                )
-            return made
+                src, dst = part.at[to], precv.at[d - 1]
+            else:
+                src, dst = send.at[to, pl.ds(0, size)], recv.at[d - 1, pl.ds(0, size)]
+            return [remote(src, dst, s_send.at[step, d - 1], s_recv.at[step, d - 1], d)]
 
         def spread(d):
             made = [
@@ -211,13 +209,10 @@
             for d in range(1, n):
                 for c in scatter(d):
                     c.wait_recv()
-                total += recv[step, d - 1, :size].astype(F32)
+                total += (recv[d - 1, :size] if step else precv[d - 1]).astype(F32)
             gath[step, me, :size] = total.astype(BF16)
             if step == 0:
-                base = bsend[me]
-                for d in range(1, n):
-                    base += brecv[d - 1]
-                bgath[me] = base
+                bgath[me] = total[cells:]
             for d in range(1, n):
                 for c in spread(d):
                     c.start()
@@ -265,42 +260,83 @@
         correction = dot(mult[:size], jnp.concatenate([base, base], axis=0))
         return (f_v[b, :size] + correction + scale * collision).astype(BF16)
 
-    acc[...] = jnp.zeros_like(acc)
-    eacc[...] = jnp.zeros_like(eacc)
-    extra = lax.broadcasted_iota(jnp.int32, (EXT, WIDTH), 0) >= FIRST
-
-    @pl.loop(0, count)
-    def _(b):
-        dens_copy(b).wait()
-        x = jnp.concatenate([p_v[b], left_ref[b // PACK], right_ref[b // PACK]], axis=0)
-        f = dot(a1_ref[b], jnp.concatenate([x, x], axis=0))
-        f_v[b] = f
-        eacc[...] += energy_of(f, b)
-        coarse = f.astype(BF16)
-        tail = jnp.where(extra, basis_ref[b].astype(F32), f[cells:]).astype(BF16)
-        coder_copy(b).wait()
-        acc[...] += dot(jnp.concatenate([coarse[:cells], tail], axis=0), coder_v[b])
+    def courant(b):
+        along = 2 * (blocks_ref[b] * WIDTH // (VGRID * VGRID)) + 1 - VGRID
+        return along.astype(F32)
+
+    def velocity_rows(b):
+        nx = courant(b)
+        ny = fixed_ref[:1] + (2 * (blocks_ref[b] * (WIDTH // VGRID) % VGRID)).astype(F32)
+        nz = fixed_ref[1:2]
+        kinetic = nx * nx + ny * ny + nz * nz
+        upper = jnp.floor(kinetic * (1.0 / 64.0)) * 64.0
+        energy_ref[b] = kinetic * (1.0 / (VGRID * VGRID))
+        full = jnp.zeros((EXT, WIDTH), F32)
+        for i, value in enumerate((1.0, nx, ny, nz, upper, kinetic - upper)):
+            full = jnp.where(extra == FIRST + i, value, full)
+        basis_ref[b] = full.astype(BF16)
+        return full
+
+    extra = lax.broadcasted_iota(jnp.int32, (EXT, WIDTH), 0)
+    unit = math.gcd(count, 2)
+    speed = COURANT / VGRID
+
+    def coder_rows(start):
+        return coder_v[pl.ds(start, unit)].reshape(unit * WIDTH, latent)
+
+    def zero():
+        acc[...] = jnp.zeros_like(acc)
+        eacc[...] = jnp.zeros_like(eacc)
+
+    zero()
+
+    @pl.loop(0, count // unit)
+    def _(g):
+        parts = []
+        for u in range(unit):
+            b = g * unit + u
+            dens_copy(b).wait()
+            x = jnp.concatenate([p_v[b], left_ref[b // PACK], right_ref[b // PACK]], axis=0)
+            group = group_ref[:1]
+            mine = (group < 0.0) | (group == (b % PACK).astype(F32))
+            weights = stencil(courant(b) * speed, jnp.where(mine, first_ref[...], 9.0))
+            f = dot(weights, jnp.concatenate([x, x], axis=0))
+            base = velocity_rows(b)
+            f_v[b] = f
+            eacc[...] += energy_of(f, b)
+            tail = jnp.where(extra >= FIRST, base, f[cells:]).astype(BF16)
+            parts.append(jnp.concatenate([f[:cells].astype(BF16), tail], axis=0))
+        for u in range(unit):
+            coder_copy(g * unit + u).wait()
+        acc[...] += dot(jnp.concatenate(parts, axis=1), coder_rows(g * unit))
 
     latent_layer(0, rows)
-    acc[...] = jnp.zeros_like(acc)
-    eacc[...] = jnp.zeros_like(eacc)
-
-    @pl.loop(0, count)
-    def _(b):
-        state = advanced(b, rows)
-        edge = jnp.where(keep_ref[...] > 0.0, state[cells:].astype(F32), inflow_ref[b]).astype(BF16)
-        x = jnp.concatenate([state[:cells], edge], axis=0)
-        f = dot(a2_ref[b], jnp.concatenate([x, x], axis=0))
-        f_v[b, :cells] = f
-        eacc[:cells] += energy_of(f, b)
-        acc[:cells] += dot(f.astype(BF16), coder_v[b])
+    zero()
+
+    @pl.loop(0, count // unit)
+    def _(g):
+        parts = []
+        for u in range(unit):
+            b = g * unit + u
+            state = advanced(b, rows)
+            edge = jnp.where(keep_ref[...] > 0.0, state[cells:].astype(F32), inflow_ref[b])
+            x = jnp.concatenate([state[:cells], edge.astype(BF16)], axis=0)
+            weights = stencil(courant(b) * speed, second_ref[...])
+            f = dot(weights, jnp.concatenate([x, x], axis=0))
+            f_v[b, :cells] = f
+            eacc[:cells] += energy_of(f, b)
+            parts.append(f.astype(BF16))
+        acc[:cells] += dot(jnp.concatenate(parts, axis=1), coder_rows(g * unit))
 
     latent_layer(1, cells)
 
-    @pl.loop(0, count)
-    def _(b):
-        p_v[b] = advanced(b, cells)
-        out_copy(b).start()
+    @pl.loop(0, count // unit)
+    def _(g):
+        for u in range(unit):
+            b = g * unit + u
+            p_v[b] = advanced(b, cells)
+        for u in range(unit):
+            out_copy(g * unit + u).start()
 
     @pl.loop(0, count)
     def _(b):
@@ -334,23 +370,7 @@
         lax.dynamic_index_in_dim(flags, (position + 1) % block_count, 0, keepdims=False) == 1
     )
 
-    number = blocks[:, None] * WIDTH + jnp.arange(WIDTH, dtype=jnp.int32)[None, :]
-    nx = 2 * (number // (VGRID * VGRID)) + 1 - VGRID
-    ny = 2 * (number // VGRID % VGRID) + 1 - VGRID
-    nz = 2 * (number % VGRID) + 1 - VGRID
-    kinetic = nx * nx + ny * ny + nz * nz
-    upper = kinetic // 64 * 64
-    zero = jnp.zeros_like(nx)
-    basis = jnp.stack(
-        [zero] * FIRST + [zero + 1, nx, ny, nz, upper, kinetic - upper] + [zero] * (EXT - FIRST - 6),
-        axis=1,
-    ).astype(BF16)
-    energy = (kinetic.astype(F32) / (VGRID * VGRID))[:, None, :]
-    along = 2 * (blocks * WIDTH // (VGRID * VGRID)) + 1 - VGRID
-    courant = COURANT * (along.astype(F32) / VGRID)
-    first, second = offsets(cells, count)
-    a1 = stencil(courant, first)
-    a2 = stencil(courant, second)
+    first, second, group = tables(cells)
 
     def packed(ghosts, is_open):
         ghosts = jnp.where(is_open, ghosts, inflow.astype(BF16)[None])
@@ -371,29 +391,30 @@
     return pl.pallas_call(
         functools.partial(kernel, n, owners, cells, math.sqrt(VELS / latent)),
         out_shape=jax.ShapeDtypeStruct((cells, columns), BF16),
-        in_specs=[hbm, hbm] + [vmem] * 11,
+        in_specs=[pl.BlockSpec(memory_space=pltpu.SMEM), hbm, hbm] + [vmem] * 11,
         out_specs=hbm,
         scratch_shapes=[
+            pltpu.VMEM((count, EXT, WIDTH), BF16),
+            pltpu.VMEM((count, 1, WIDTH), F32),
             pltpu.VMEM((count, WIDTH, latent), BF16),
             pltpu.VMEM((count, cells, WIDTH), BF16),
             pltpu.VMEM((count, rows, WIDTH), F32),
             pltpu.VMEM((rows, latent), F32),
             pltpu.VMEM((rows, 128), F32),
-            pltpu.VMEM((2, owners, rows, piece), BF16),
-            pltpu.VMEM((2, others, rows, piece), BF16),
+            pltpu.VMEM((owners, rows, piece), BF16),
+            pltpu.VMEM((others, rows, piece), BF16),
             pltpu.VMEM((owners, rows, piece), F32),
+            pltpu.VMEM((others, rows, piece), F32),
             pltpu.VMEM((2, owners, rows, piece), BF16),
             pltpu.VMEM((2, 8, 128), F32),
             pltpu.VMEM((2, others, 8, 128), F32),
-            pltpu.VMEM((owners, EXT, piece), F32),
-            pltpu.VMEM((others, EXT, piece), F32),
             pltpu.VMEM((owners, EXT, piece), F32),
             pltpu.VMEM((rows, 2 * EXT), BF16),
             pltpu.VMEM((rows, latent), BF16),
             dma((count,)), dma((count,)), dma((count,)),
             dma((2, others)), dma((2, others)), dma((2, others)), dma((2, owners)),
             dma((2, others)), dma((2, others)),
-            dma((others,)), dma((others,)), dma((others,)), dma((owners,)),
+            dma((others,)), dma((owners,)),
         ],
         compiler_params=pltpu.CompilerParams(
             collective_id=0, has_side_effects=True, vmem_limit_bytes=60 * 1024 * 1024
@@ -402,8 +423,8 @@
             flops=flops, bytes_accessed=2 * columns * (latent + 2 * cells), transcendentals=0
         ),
     )(
-        coder.reshape(count, WIDTH, latent), density,
-        packed(left, open_left), packed(right, open_right), basis, a1, a2, energy,
+        blocks, coder.reshape(count, WIDTH, latent), density,
+        packed(left, open_left), packed(right, open_right), first, second, group, fixed_rows(),
         inflow.reshape(count, 1, WIDTH), keep[:, None], w_latent, b_latent[None, :], rest[:, None],
     )
 

time: 112 us -> 94 us (0.84)
  other arithmetic: 13.1 us -> 2.46 us
  Pallas kernels: 79.4 us -> 74 us
  local copies, waits for them, and re-layouts: 14.2 us -> 11 us
  waiting for transfers between devices: 0.01 us -> 1.77 us
    pallas_call x1, Pallas kernels: 79.4 us -> 74 us  [body(): pl.pallas_call(functools.partial(kernel, n, owners, cells, math.sqrt(VELS...]
    another operation x5 -> x1, local copies, waits for them, and re-layouts: 3.99 us -> 0.01 us  [the longest x3 3.93 us: body(): jnp.stack([zero] * FIRST + [zero + 1, nx, ny, nz, upper, kinetic - upper]...]
    another operation x1 -> x0, other arithmetic: 3.13 us -> none
    div x1 -> x0, other arithmetic: 2.97 us -> none  [body(): energy = (kinetic.astype(F32) / (VGRID * VGRID))[:, None, :]]
    concatenate x2 -> x0, other arithmetic: 2.82 us -> none  [stencil(): return jnp.concatenate([high, low], axis=2)]
    convert_element_type x2 -> x0, other arithmetic: 1.95 us -> none  [the longest x1 1.17 us: stencil(): low = (full - high.astype(F32)).astype(BF16)]
    ppermute x4, waiting for transfers between devices: 0.01 us -> 1.77 us  [ring(): lax.ppermute(value, ('cell', 'sub'), [(i, (i + step) % count) for i in ra...]
    unnamed x27 -> x1, local copies, waits for them, and re-layouts: 5.29 us -> 5.23 us
  transfers between devices with their start and end apart: 4 -> 4, of which waited for: 0 -> 1; matrix products, arithmetic and copies ran while one was open for 18% -> 6% of each run, Pallas kernels for 0% -> 0%
where the time goes in v2:
time: 94 us; the launch traced here: 93.7 us
  Pallas kernels  74 us (79%)
  local copies, waits for them, and re-layouts  11 us (12%)
  starting transfers between devices  3.17 us (3%)
  other arithmetic  2.46 us (3%)
  waiting for transfers between devices  1.77 us (2%)
  between operations  1.36 us (1%)
    pallas_call x1, Pallas kernels, body(): pl.pallas_call(functools.partial(kernel, n, owners, cells, math.sqrt(VELS...  74 us
    unnamed x1, local copies, waits for them, and re-layouts  5.23 us
    ppermute x4, starting transfers between devices, ring(): lax.ppermute(value, ('cell', 'sub'), [(i, (i + step) % count) for i in ra...  3.17 us
  transfers between devices with their start and end apart: 4, of which 1 were waited for; matrix products, arithmetic and copies ran while one was open for 6% of the time, Pallas kernels for 0%

profile of v2, /device:TPU:0, one launch (start us, length us, event | category | flops | bytes accessed | tf_op | source)
XLA Modules:
  0.0 93.7 jit_solution(16847403793883938242)
XLA Ops:
  0.0 0.8 fusion.4
  0.8 0.5 collective-permute-start.2
  1.3 1.9 %collective-permute-start.3 = (f32[2]{0:T(128)S(1)}, f32[2]{0:T(128)S(1)}, u32[]{:S(2)}, u32[]{:S(2)}) collective-permute-start(f32[2]{0:T(128)S(1)} %get-tuple-element.10), channel_id=1, source_target_pairs={{0,3},{1,0},{2,1},{3,2},{4,7},{5,4},{6,5},{7,6},{8,11},{9,8},{10,9... | collective-permute-start | bytes 32 | tf_op jit(solution)/shard_map/ppermute | solution.py:348
  3.2 1.3 %fusion.3 = (bf16[4,27648]{1,0:T(4,128)(2,1)S(1)}, bf16[4,27648]{1,0:T(4,128)(2,1)S(1)}) fusion(bf16[96,27648]{1,0:T(8,128)(2,1)} %dens_hbm.1), kind=kLoop, calls=%fused_computation.8 | loop fusion | bytes 884736 | tf_op jit(solution)/shard_map/slice | solution.py:361
  4.5 0.7 collective-permute-start.1
  5.2 0.1 collective-permute-start
  5.3 1.4 %fusion.5 = (s32[1]{0:T(128)}, s32[1]{0:T(128)}) fusion(s32[4]{0:T(128)} %param.18, s32[]{:T(128)S(6)} %select_n.54, s32[]{:T(128)S(6)} %select_n.50), kind=kLoop, calls=%fused_computation.10 | loop fusion | bytes 24 | tf_op jit(solution)/shard_map/jit(dynamic_index_in_dim)/dynamic_slice | solution.py:370
  8.0 0.9 convert_element_type.14
  8.9 0.6 fusion.1.keep_ref
  9.5 0.0 collective-permute-done.2
  9.5 0.0 collective-permute-done.3
  9.5 0.7 maximum_bitcast_fusion
  10.3 0.7 copy.15.rest_ref
  11.0 0.0 collective-permute-done.1
  11.0 1.8 %collective-permute-done = bf16[4,27648]{1,0:T(4,128)(2,1)S(1)} collective-permute-done((bf16[4,27648]{1,0:T(4,128)(2,1)S(1)}, bf16[4,27648]{1,0:T(4,128)(2,1)S(1)}, u32[]{:S(2)}, u32[]{:S(2)}) %collective-permute-start) | collective-permute-done | bytes 221216 | tf_op jit(solution)/shard_map/ppermute | solution.py:348
  12.8 0.2 broadcast_select_fusion
  13.0 0.8 reshape.49.right_ref
  13.8 0.7 reshape.47.left_ref
  14.5 74.0 %shard_map.118 = bf16[96,27648]{1,0:T(8,128)(2,1)} custom-call(s32[24]{0:T(128)} %blocks_ref.1, bf16[24,1152,512]{2,1,0:T(8,128)(2,1)} %bitcast.16, bf16[96,27648]{1,0:T(8,128)(2,1)} %dens_hbm.1, bf16[6,16,1152]{2,1,0:T(8,128)(2,1)} %reshape.47.left_ref, bf16[6,16,1152]{2,1,0:T(8,128)(2,1)} %reshape.49.right_ref, f32[112,128]{1,0:T(8,128)} %constant.47.clone.first_ref, ...), custom_call_target="tpu_custom_call" | custom-call | flops 15854469120 | bytes 38928384 | tf_op jit(solution)/shard_map/pallas_call | solution.py:391
  88.5 5.2 %copy.17 = bf16[96,27648]{1,0:T(8,128)(2,1)} copy(bf16[96,27648]{1,0:T(8,128)(2,1)} %shard_map.118) | data formatting | bytes 10616832
  (1 shorter events, 0.0 us)
Async XLA Ops:
  0.8 8.7 %collective-permute-start.2 = (f32[2]{0:T(128)S(1)}, f32[2]{0:T(128)S(1)}, u32[]{:S(2)}, u32[]{:S(2)}) collective-permute-start(f32[2]{0:T(128)S(1)} %get-tuple-element.9), channel_id=1, source_target_pairs={{0,1},{1,2},{2,3},{3,0},{4,5},{5,6},{6,7},{7,4},{8,9},{9,10},{10,1... | collective-permute-start | bytes 32 | tf_op jit(solution)/shard_map/ppermute | solution.py:348
  1.3 8.3 %collective-permute-start.3 = (f32[2]{0:T(128)S(1)}, f32[2]{0:T(128)S(1)}, u32[]{:S(2)}, u32[]{:S(2)}) collective-permute-start(f32[2]{0:T(128)S(1)} %get-tuple-element.10), channel_id=1, source_target_pairs={{0,3},{1,0},{2,1},{3,2},{4,7},{5,4},{6,5},{7,6},{8,11},{9,8},{10,9... | collective-permute-start | bytes 32 | tf_op jit(solution)/shard_map/ppermute | solution.py:348
  4.5 6.5 %collective-permute-start.1 = (bf16[4,27648]{1,0:T(4,128)(2,1)S(1)}, bf16[4,27648]{1,0:T(4,128)(2,1)S(1)}, u32[]{:S(2)}, u32[]{:S(2)}) collective-permute-start(bf16[4,27648]{1,0:T(4,128)(2,1)S(1)} %get-tuple-element.5), channel_id=1, source_target_pairs={{0,3},{1,0},{2,1},{3,2},{4,7},{5,4},{6,5},{7,6},{8,11},{9,8},{10,9... | collective-permute-start | bytes 663560 | tf_op jit(solution)/shard_map/ppermute | solution.py:348
  5.2 7.5 %collective-permute-start = (bf16[4,27648]{1,0:T(4,128)(2,1)S(1)}, bf16[4,27648]{1,0:T(4,128)(2,1)S(1)}, u32[]{:S(2)}, u32[]{:S(2)}) collective-permute-start(bf16[4,27648]{1,0:T(4,128)(2,1)S(1)} %get-tuple-element.6), channel_id=1, source_target_pairs={{0,1},{1,2},{2,3},{3,0},{4,5},{5,6},{6,7},{7,4},{8,9},{9,10},{10,1... | collective-permute-start | bytes 663560 | tf_op jit(solution)/shard_map/ppermute | solution.py:348

commit v3 on v2

--- a/solution.py
+++ b/solution.py
@@ -235,7 +235,7 @@
         energy_sum = exchange(step, size)
         encoded = jnp.concatenate([gath[step, q, :size] for q in range(owners)], axis=1)
         active = jnp.tanh(dot(encoded, w_ref[...]) + bias_ref[...]).astype(BF16)
-        act_v[:size] = active
+        act_v[:, :size] = active.astype(F32).T.astype(BF16)
         base = jnp.concatenate([bgath[q] for q in range(owners)], axis=1)
         sums = scale * dot_t(active.astype(F32), base, precision=lax.Precision.HIGHEST)
         total, cross, quartic, square = grid_moments()
@@ -256,7 +256,7 @@
 
     def advanced(b, size):
         base = basis_ref[b]
-        collision = dot_t(act_v[:size], coder_v[b])
+        collision = dot(coder_v[b], act_v[...]).T[:size]
         correction = dot(mult[:size], jnp.concatenate([base, base], axis=0))
         return (f_v[b, :size] + correction + scale * collision).astype(BF16)
 
@@ -283,6 +283,8 @@
 
     def coder_rows(start):
         return coder_v[pl.ds(start, unit)].reshape(unit * WIDTH, latent)
+
+    act_v[...] = jnp.zeros_like(act_v)
 
     def zero():
         acc[...] = jnp.zeros_like(acc)
@@ -410,7 +412,7 @@
             pltpu.VMEM((2, others, 8, 128), F32),
             pltpu.VMEM((owners, EXT, piece), F32),
             pltpu.VMEM((rows, 2 * EXT), BF16),
-            pltpu.VMEM((rows, latent), BF16),
+            pltpu.VMEM((latent, -(-rows // 128) * 128), BF16),
             dma((count,)), dma((count,)), dma((count,)),
             dma((2, others)), dma((2, others)), dma((2, others)), dma((2, owners)),
             dma((2, others)), dma((2, others)),

time: 94 us -> 99.5 us (1.059)
  Pallas kernels: 74 us -> 79.4 us
    pallas_call x1, Pallas kernels: 74 us -> 79.4 us  [body(): pl.pallas_call(functools.partial(kernel, n, owners, cells, math.sqrt(VELS...]
where the time goes in v3:
time: 99.5 us; the launch traced here: 99.2 us
  Pallas kernels  79.4 us (80%)
  local copies, waits for them, and re-layouts  11 us (11%)
  starting transfers between devices  3.17 us (3%)
  other arithmetic  2.46 us (2%)
  waiting for transfers between devices  1.77 us (2%)
  between operations  1.36 us (1%)
    pallas_call x1, Pallas kernels, body(): pl.pallas_call(functools.partial(kernel, n, owners, cells, math.sqrt(VELS...  79.4 us
    unnamed x1, local copies, waits for them, and re-layouts  5.23 us
    ppermute x4, starting transfers between devices, ring(): lax.ppermute(value, ('cell', 'sub'), [(i, (i + step) % count) for i in ra...  3.17 us
  transfers between devices with their start and end apart: 4, of which 1 were waited for; matrix products, arithmetic and copies ran while one was open for 6% of the time, Pallas kernels for 0%

profile of v3, /device:TPU:0, one launch (start us, length us, event | category | flops | bytes accessed | tf_op | source)
XLA Modules:
  0.0 99.2 jit_solution(5931614104143816968)
XLA Ops:
  0.0 0.8 fusion.4
  0.8 0.5 collective-permute-start.2
  1.3 1.9 %collective-permute-start.3 = (f32[2]{0:T(128)S(1)}, f32[2]{0:T(128)S(1)}, u32[]{:S(2)}, u32[]{:S(2)}) collective-permute-start(f32[2]{0:T(128)S(1)} %get-tuple-element.10), channel_id=1, source_target_pairs={{0,3},{1,0},{2,1},{3,2},{4,7},{5,4},{6,5},{7,6},{8,11},{9,8},{10,9... | collective-permute-start | bytes 32 | tf_op jit(solution)/shard_map/ppermute | solution.py:350
  3.2 1.3 %fusion.3 = (bf16[4,27648]{1,0:T(4,128)(2,1)S(1)}, bf16[4,27648]{1,0:T(4,128)(2,1)S(1)}) fusion(bf16[96,27648]{1,0:T(8,128)(2,1)} %dens_hbm.1), kind=kLoop, calls=%fused_computation.8 | loop fusion | bytes 884736 | tf_op jit(solution)/shard_map/slice | solution.py:363
  4.5 0.7 collective-permute-start.1
  5.2 0.1 collective-permute-start
  5.3 1.4 %fusion.5 = (s32[1]{0:T(128)}, s32[1]{0:T(128)}) fusion(s32[4]{0:T(128)} %param.18, s32[]{:T(128)S(6)} %select_n.54, s32[]{:T(128)S(6)} %select_n.50), kind=kLoop, calls=%fused_computation.10 | loop fusion | bytes 24 | tf_op jit(solution)/shard_map/jit(dynamic_index_in_dim)/dynamic_slice | solution.py:372
  8.0 0.9 convert_element_type.14
  8.9 0.6 fusion.1.keep_ref
  9.5 0.0 collective-permute-done.2
  9.5 0.0 collective-permute-done.3
  9.5 0.7 maximum_bitcast_fusion
  10.3 0.7 copy.15.rest_ref
  11.0 0.0 collective-permute-done.1
  11.0 1.8 %collective-permute-done = bf16[4,27648]{1,0:T(4,128)(2,1)S(1)} collective-permute-done((bf16[4,27648]{1,0:T(4,128)(2,1)S(1)}, bf16[4,27648]{1,0:T(4,128)(2,1)S(1)}, u32[]{:S(2)}, u32[]{:S(2)}) %collective-permute-start) | collective-permute-done | bytes 221216 | tf_op jit(solution)/shard_map/ppermute | solution.py:350
  12.8 0.2 broadcast_select_fusion
  13.0 0.8 reshape.49.right_ref
  13.8 0.7 reshape.47.left_ref
  14.5 79.4 %shard_map.118 = bf16[96,27648]{1,0:T(8,128)(2,1)} custom-call(s32[24]{0:T(128)} %blocks_ref.1, bf16[24,1152,512]{2,1,0:T(8,128)(2,1)} %bitcast.16, bf16[96,27648]{1,0:T(8,128)(2,1)} %dens_hbm.1, bf16[6,16,1152]{2,1,0:T(8,128)(2,1)} %reshape.47.left_ref, bf16[6,16,1152]{2,1,0:T(8,128)(2,1)} %reshape.49.right_ref, f32[112,128]{1,0:T(8,128)} %constant.47.clone.first_ref, ...), custom_call_target="tpu_custom_call" | custom-call | flops 15854469120 | bytes 38928384 | tf_op jit(solution)/shard_map/pallas_call | solution.py:393
  94.0 5.2 %copy.17 = bf16[96,27648]{1,0:T(8,128)(2,1)} copy(bf16[96,27648]{1,0:T(8,128)(2,1)} %shard_map.118) | data formatting | bytes 10616832
  (1 shorter events, 0.0 us)
Async XLA Ops:
  0.8 8.7 %collective-permute-start.2 = (f32[2]{0:T(128)S(1)}, f32[2]{0:T(128)S(1)}, u32[]{:S(2)}, u32[]{:S(2)}) collective-permute-start(f32[2]{0:T(128)S(1)} %get-tuple-element.9), channel_id=1, source_target_pairs={{0,1},{1,2},{2,3},{3,0},{4,5},{5,6},{6,7},{7,4},{8,9},{9,10},{10,1... | collective-permute-start | bytes 32 | tf_op jit(solution)/shard_map/ppermute | solution.py:350
  1.3 8.3 %collective-permute-start.3 = (f32[2]{0:T(128)S(1)}, f32[2]{0:T(128)S(1)}, u32[]{:S(2)}, u32[]{:S(2)}) collective-permute-start(f32[2]{0:T(128)S(1)} %get-tuple-element.10), channel_id=1, source_target_pairs={{0,3},{1,0},{2,1},{3,2},{4,7},{5,4},{6,5},{7,6},{8,11},{9,8},{10,9... | collective-permute-start | bytes 32 | tf_op jit(solution)/shard_map/ppermute | solution.py:350
  4.5 6.5 %collective-permute-start.1 = (bf16[4,27648]{1,0:T(4,128)(2,1)S(1)}, bf16[4,27648]{1,0:T(4,128)(2,1)S(1)}, u32[]{:S(2)}, u32[]{:S(2)}) collective-permute-start(bf16[4,27648]{1,0:T(4,128)(2,1)S(1)} %get-tuple-element.5), channel_id=1, source_target_pairs={{0,3},{1,0},{2,1},{3,2},{4,7},{5,4},{6,5},{7,6},{8,11},{9,8},{10,9... | collective-permute-start | bytes 663560 | tf_op jit(solution)/shard_map/ppermute | solution.py:350
  5.2 7.5 %collective-permute-start = (bf16[4,27648]{1,0:T(4,128)(2,1)S(1)}, bf16[4,27648]{1,0:T(4,128)(2,1)S(1)}, u32[]{:S(2)}, u32[]{:S(2)}) collective-permute-start(bf16[4,27648]{1,0:T(4,128)(2,1)S(1)} %get-tuple-element.6), channel_id=1, source_target_pairs={{0,1},{1,2},{2,3},{3,0},{4,5},{5,6},{6,7},{7,4},{8,9},{9,10},{10,1... | collective-permute-start | bytes 663560 | tf_op jit(solution)/shard_map/ppermute | solution.py:350

commit v4 on v2

--- a/solution.py
+++ b/solution.py
@@ -92,13 +92,20 @@
 
 def kernel(
     n, owners, cells, scale,
-    blocks_ref, coder_hbm, dens_hbm, left_ref, right_ref, first_ref, second_ref, group_ref, fixed_ref,
-    inflow_ref, keep_ref, w_ref, bias_ref, rest_ref,
+    blocks_ref, flags_ref, coder_hbm, dens_hbm, first_ref, second_ref, group_ref, fixed_ref,
+    inflow_ref, w_ref, bias_ref, rest_ref,
     out_hbm,
+    to_right, to_left, left_ref, right_ref, rest_left, rest_right, h_send, h_recv, r_send, r_recv,
     basis_ref, energy_ref, coder_v, p_v, f_v, acc, eacc, send, recv, part, precv, gath, esend, erecv, bgath, mult, act_v,
     coder_sem, dens_sem, out_sem, s_send, s_recv, g_send, g_recv, e_send, e_recv, c_send, c_recv,
 ):
     me = lax.axis_index("vel")
+    subs = lax.axis_size("sub")
+    ring = lax.axis_size("cell") * subs
+    place = lax.axis_index("cell") * subs + lax.axis_index("sub")
+    next_place, last_place = lax.rem(place + 1, ring), lax.rem(place + ring - 1, ring)
+    on_right = {"cell": next_place // subs, "sub": lax.rem(next_place, subs)}
+    on_left = {"cell": last_place // subs, "sub": lax.rem(last_place, subs)}
     count = coder_v.shape[0]
     rows = cells + EXT
     latent = coder_v.shape[2]
@@ -119,6 +126,9 @@
     @pl.loop(0, count)
     def _(b):
         dens_copy(b).start()
+
+    @pl.loop(0, count)
+    def _(b):
         coder_copy(b).start()
 
     barrier = pltpu.get_barrier_semaphore()
@@ -126,7 +136,65 @@
         pl.semaphore_signal(
             barrier, inc=1, device_id={"vel": lax.rem(me + d, n)}, device_id_type=MESH
         )
-    pl.semaphore_wait(barrier, n - 1)
+    for neighbour in (on_left, on_right):
+        pl.semaphore_signal(barrier, inc=1, device_id=neighbour, device_id_type=MESH)
+    pl.semaphore_wait(barrier, n + 1)
+
+    pack = min(PACK, count)
+    chunks = count // pack
+
+    def halo_copies(c):
+        return [
+            pltpu.make_async_remote_copy(
+                src_ref=src.at[c], dst_ref=dst.at[c], send_sem=h_send.at[i, c],
+                recv_sem=h_recv.at[i, c], device_id=to, device_id_type=MESH,
+            )
+            for i, (src, dst, to) in enumerate(
+                ((to_right, left_ref, on_right), (to_left, right_ref, on_left))
+            )
+        ]
+
+    def rest_copies():
+        return [
+            pltpu.make_async_remote_copy(
+                src_ref=rest_ref, dst_ref=dst, send_sem=r_send.at[i],
+                recv_sem=r_recv.at[i], device_id=to, device_id_type=MESH,
+            )
+            for i, (dst, to) in enumerate(((rest_left, on_right), (rest_right, on_left)))
+        ]
+
+    for copy in rest_copies():
+        copy.start()
+
+    pick_row = lax.broadcasted_iota(jnp.int32, (4 * PACK, 16 * pack), 0)
+    pick_col = lax.broadcasted_iota(jnp.int32, (4 * PACK, 16 * pack), 1)
+    pick = (pick_row // 4) * 16 + pick_row % 4
+    pick_head = jnp.where(pick_col == pick, 1.0, 0.0).astype(BF16)
+    pick_tail = jnp.where(pick_col == pick + 12, 1.0, 0.0).astype(BF16)
+
+    @pl.loop(0, chunks)
+    def _(c):
+        for u in range(pack):
+            dens_copy(c * pack + u).wait()
+        heads = jnp.concatenate([p_v[c * pack + u, :16] for u in range(pack)], axis=0)
+        tails = jnp.concatenate([p_v[c * pack + u, cells - 16 :] for u in range(pack)], axis=0)
+        to_left[c] = dot(pick_head, heads).astype(BF16)
+        to_right[c] = dot(pick_tail, tails).astype(BF16)
+        for copy in halo_copies(c):
+            copy.start()
+
+    open_left = flags_ref[place].astype(F32)
+    open_right = flags_ref[next_place].astype(F32)
+
+    def rest_column(size):
+        eye = lax.broadcasted_iota(jnp.int32, (size, 128), 0) == lax.broadcasted_iota(
+            jnp.int32, (size, 128), 1
+        )
+        lane = lax.broadcasted_iota(jnp.int32, (1, 128), 1)
+        row = jnp.where(lane < cells, rest_ref[:1], 0.0)
+        row = jnp.where((lane >= cells) & (lane < cells + 2), rest_left[1:2], row)
+        row = jnp.where((lane >= cells + 2) & (lane < cells + 4), rest_right[2:3], row)
+        return jnp.sum(jnp.where(eye, row, 0.0), axis=1, keepdims=True)
 
     def only(test, run):
         if n == owners:
@@ -239,7 +307,11 @@
         base = jnp.concatenate([bgath[q] for q in range(owners)], axis=1)
         sums = scale * dot_t(active.astype(F32), base, precision=lax.Precision.HIGHEST)
         total, cross, quartic, square = grid_moments()
-        sink = -SINK_RATE * (1.0 - rest_ref[:size] * rest_ref[:size]) * energy_sum
+        if step == 0:
+            for copy in rest_copies():
+                copy.wait()
+        rest = rest_column(size)
+        sink = -SINK_RATE * (1.0 - rest * rest) * energy_sum
         grid = float(VGRID)
         m = [sums[:, FIRST + i : FIRST + i + 1] for i in range(6)]
         excess = (m[4] + m[5]) / (grid * grid) - sink
@@ -278,8 +350,10 @@
         return full
 
     extra = lax.broadcasted_iota(jnp.int32, (EXT, WIDTH), 0)
-    unit = math.gcd(count, 2)
+    unit = math.gcd(pack, 2)
     speed = COURANT / VGRID
+
+    keep = jnp.where(extra < 2, open_left, jnp.where(extra < 4, open_right, 1.0))
 
     def coder_rows(start):
         return coder_v[pl.ds(start, unit)].reshape(unit * WIDTH, latent)
@@ -290,15 +364,21 @@
 
     zero()
 
-    @pl.loop(0, count // unit)
-    def _(g):
+    @pl.loop(0, chunks)
+    def _(c):
+        for copy in halo_copies(c):
+            copy.wait()
         parts = []
-        for u in range(unit):
-            b = g * unit + u
-            dens_copy(b).wait()
-            x = jnp.concatenate([p_v[b], left_ref[b // PACK], right_ref[b // PACK]], axis=0)
+        for u in range(pack):
+            b = c * pack + u
+            inflow = jnp.broadcast_to(inflow_ref[b], (4 * PACK, WIDTH))
+            ghosts = [
+                jnp.where(jnp.full((4 * PACK, WIDTH), is_open) > 0.0, held[c].astype(F32), inflow)
+                for held, is_open in ((left_ref, open_left), (right_ref, open_right))
+            ]
+            x = jnp.concatenate([p_v[b]] + [g.astype(BF16) for g in ghosts], axis=0)
             group = group_ref[:1]
-            mine = (group < 0.0) | (group == (b % PACK).astype(F32))
+            mine = (group < 0.0) | (group == float(u))
             weights = stencil(courant(b) * speed, jnp.where(mine, first_ref[...], 9.0))
             f = dot(weights, jnp.concatenate([x, x], axis=0))
             base = velocity_rows(b)
@@ -306,9 +386,12 @@
             eacc[...] += energy_of(f, b)
             tail = jnp.where(extra >= FIRST, base, f[cells:]).astype(BF16)
             parts.append(jnp.concatenate([f[:cells].astype(BF16), tail], axis=0))
-        for u in range(unit):
-            coder_copy(g * unit + u).wait()
-        acc[...] += dot(jnp.concatenate(parts, axis=1), coder_rows(g * unit))
+            if len(parts) == unit:
+                start = b + 1 - unit
+                for v in range(unit):
+                    coder_copy(start + v).wait()
+                acc[...] += dot(jnp.concatenate(parts, axis=1), coder_rows(start))
+                parts = []
 
     latent_layer(0, rows)
     zero()
@@ -319,7 +402,8 @@
         for u in range(unit):
             b = g * unit + u
             state = advanced(b, rows)
-            edge = jnp.where(keep_ref[...] > 0.0, state[cells:].astype(F32), inflow_ref[b])
+            inflow = jnp.broadcast_to(inflow_ref[b], (EXT, WIDTH))
+            edge = jnp.where(keep > 0.0, state[cells:].astype(F32), inflow)
             x = jnp.concatenate([state[:cells], edge.astype(BF16)], axis=0)
             weights = stencil(courant(b) * speed, second_ref[...])
             f = dot(weights, jnp.concatenate([x, x], axis=0))
@@ -343,46 +427,24 @@
         out_copy(b).wait()
 
 
-def ring(value, step):
-    count = lax.axis_size("cell") * lax.axis_size("sub")
-    return lax.ppermute(value, ("cell", "sub"), [(i, (i + step) % count) for i in range(count)])
-
-
 def body(density, coder, w_latent, b_latent, restitution, inflow, flags, blocks):
     cells, columns = density.shape
     latent = coder.shape[1]
     count = columns // WIDTH
     chunks = -(-count // PACK)
+    ghost = pltpu.VMEM((chunks, 4 * PACK, WIDTH), BF16)
     n = lax.axis_size("vel")
     owners = min(n, latent // 128)
     rows = cells + EXT
 
-    left = ring(density[-4:], 1)
-    right = ring(density[:4], -1)
-    rest_left = ring(restitution[-2:], 1)
-    rest_right = ring(restitution[:2], -1)
-
-    sub_count = lax.axis_size("sub")
-    position = lax.axis_index("cell") * sub_count + lax.axis_index("sub")
-    block_count = lax.axis_size("cell") * sub_count
-    open_left = lax.dynamic_index_in_dim(flags, position, 0, keepdims=False) == 1
-    open_right = (
-        lax.dynamic_index_in_dim(flags, (position + 1) % block_count, 0, keepdims=False) == 1
-    )
-
     first, second, group = tables(cells)
 
-    def packed(ghosts, is_open):
-        ghosts = jnp.where(is_open, ghosts, inflow.astype(BF16)[None])
-        ghosts = ghosts.reshape(4, count, WIDTH).transpose(1, 0, 2)
-        ghosts = jnp.pad(ghosts, ((0, chunks * PACK - count), (0, 0), (0, 0)))
-        return ghosts.reshape(chunks, PACK * 4, WIDTH)
-
-    rest = jnp.concatenate([restitution, rest_left, rest_right, jnp.zeros((EXT - 4,), F32)])
-    side = jnp.arange(EXT)
-    keep = jnp.where(side < 2, open_left, jnp.where(side < 4, open_right, True)).astype(F32)
+    rest = jnp.zeros((8, 128), F32).at[0, :cells].set(restitution)
+    rest = rest.at[1, cells : cells + 2].set(restitution[-2:])
+    rest = rest.at[2, cells + 2 : cells + 4].set(restitution[:2])
 
     vmem = pl.BlockSpec(memory_space=pltpu.VMEM)
+    smem = pl.BlockSpec(memory_space=pltpu.SMEM)
     hbm = pl.BlockSpec(memory_space=pl.ANY)
     dma = pltpu.SemaphoreType.DMA
     piece = latent // owners
@@ -391,9 +453,11 @@
     return pl.pallas_call(
         functools.partial(kernel, n, owners, cells, math.sqrt(VELS / latent)),
         out_shape=jax.ShapeDtypeStruct((cells, columns), BF16),
-        in_specs=[pl.BlockSpec(memory_space=pltpu.SMEM), hbm, hbm] + [vmem] * 11,
+        in_specs=[smem, smem, hbm, hbm] + [vmem] * 8,
         out_specs=hbm,
         scratch_shapes=[
+            ghost, ghost, ghost, ghost, pltpu.VMEM((8, 128), F32), pltpu.VMEM((8, 128), F32),
+            dma((2, chunks)), dma((2, chunks)), dma((2,)), dma((2,)),
             pltpu.VMEM((count, EXT, WIDTH), BF16),
             pltpu.VMEM((count, 1, WIDTH), F32),
             pltpu.VMEM((count, WIDTH, latent), BF16),
@@ -423,9 +487,8 @@
             flops=flops, bytes_accessed=2 * columns * (latent + 2 * cells), transcendentals=0
         ),
     )(
-        blocks, coder.reshape(count, WIDTH, latent), density,
-        packed(left, open_left), packed(right, open_right), first, second, group, fixed_rows(),
-        inflow.reshape(count, 1, WIDTH), keep[:, None], w_latent, b_latent[None, :], rest[:, None],
+        blocks, flags, coder.reshape(count, WIDTH, latent), density, first, second, group, fixed_rows(),
+        inflow.reshape(count, 1, WIDTH), w_latent, b_latent[None, :], rest,
     )
 
 

time: 94 us -> 82.7 us (0.88)
  local copies, waits for them, and re-layouts: 11 us -> 7.76 us
  starting transfers between devices: 3.17 us -> 0 us
  other arithmetic: 2.46 us -> 0 us
  waiting for transfers between devices: 1.77 us -> 0 us
  between operations: 1.36 us -> 0.02 us
    ppermute x4 -> x0, starting transfers between devices: 3.17 us -> none  [ring(): lax.ppermute(value, ('cell', 'sub'), [(i, (i + step) % count) for i in ra...]
    slice x2 -> x0, local copies, waits for them, and re-layouts: 2.12 us -> none  [the longest x1 1.32 us: body(): right = ring(density[:4], -1)]
    ppermute x4 -> x0, waiting for transfers between devices: 1.77 us -> none  [ring(): lax.ppermute(value, ('cell', 'sub'), [(i, (i + step) % count) for i in ra...]
    reshape x2 -> x0, local copies, waits for them, and re-layouts: 1.5 us -> none  [packed(): return ghosts.reshape(chunks, PACK * 4, WIDTH)]
    convert_element_type x2 -> x0, other arithmetic: 1.5 us -> none  [the longest x1 0.91 us: packed(): ghosts = jnp.where(is_open, ghosts, inflow.astype(BF16)[None])]
    dynamic_slice x1 -> x0, local copies, waits for them, and re-layouts: 1.39 us -> none  [body(): lax.dynamic_index_in_dim(flags, (position + 1) % block_count, 0, keepdims...]
    scatter x0 -> x3, local copies, waits for them, and re-layouts: none -> 1.14 us  [the longest x1 0.66 us: body(): rest = jnp.zeros((8, 128), F32).at[0, :cells].set(restitution)]
    unnamed x1 -> x3, local copies, waits for them, and re-layouts: 5.23 us -> 5.82 us
  transfers between devices with their start and end apart: 4 -> 0, of which waited for: 1 -> 0; matrix products, arithmetic and copies ran while one was open for 6% -> 0% of each run, Pallas kernels for 0% -> 0%
where the time goes in v4:
time: 82.7 us; the launch traced here: 82.6 us
  Pallas kernels  74.8 us (90%)
  local copies, waits for them, and re-layouts  7.76 us (9%)
    pallas_call x1, Pallas kernels, body(): pl.pallas_call(functools.partial(kernel, n, owners, cells, math.sqrt(VELS...  74.8 us
    unnamed x3, local copies, waits for them, and re-layouts  5.82 us

profile of v4, /device:TPU:0, one launch (start us, length us, event | category | flops | bytes accessed | tf_op | source)
XLA Modules:
  0.0 82.6 jit_solution(14022638801810360875)
XLA Ops:
  0.0 0.8 slice_bitcast_fusion
  0.8 0.7 scatter.10
  1.5 0.2 scatter.11
  1.7 0.3 scatter.14.rest_ref
  1.9 0.0 copy-start
  2.0 0.6 copy-done
  2.5 74.8 %shard_map.118 = bf16[96,27648]{1,0:T(8,128)(2,1)} custom-call(s32[24]{0:T(128)} %blocks_ref.1, s32[4]{0:T(128)} %flags_ref.1, bf16[24,1152,512]{2,1,0:T(8,128)(2,1)} %bitcast.9, bf16[96,27648]{1,0:T(8,128)(2,1)} %dens_hbm.1, f32[112,128]{1,0:T(8,128)} %constant.93.clone.first_ref, f32[96,112]{1,0:T(8,128)} %constant.94.clone.second_ref, ...), custom_call_target="tpu_custom_call" | custom-call | flops 15854469120 | bytes 38928384 | tf_op jit(solution)/shard_map/pallas_call | solution.py:453
  77.3 5.2 %copy.16 = bf16[96,27648]{1,0:T(8,128)(2,1)} copy(bf16[96,27648]{1,0:T(8,128)(2,1)} %shard_map.118) | data formatting | bytes 10616832
Async XLA Ops:
  1.9 0.6 copy-start

commit v5 on v4

--- a/solution.py
+++ b/solution.py
@@ -96,7 +96,7 @@
     inflow_ref, w_ref, bias_ref, rest_ref,
     out_hbm,
     to_right, to_left, left_ref, right_ref, rest_left, rest_right, h_send, h_recv, r_send, r_recv,
-    basis_ref, energy_ref, coder_v, p_v, f_v, acc, eacc, send, recv, part, precv, gath, esend, erecv, bgath, mult, act_v,
+    basis_ref, energy_ref, coder_v, p_v, f_v, acc, eacc, send, recv, part, precv, gath, esend, erecv, bgath, act_v,
     coder_sem, dens_sem, out_sem, s_send, s_recv, g_send, g_recv, e_send, e_recv, c_send, c_recv,
 ):
     me = lax.axis_index("vel")
@@ -209,7 +209,7 @@
             total += f[:, g : g + 128] * e[:, g : g + 128]
         return total
 
-    def exchange(step, size):
+    def exchange(step, size, between):
         col = jnp.sum(eacc[:size], axis=1, keepdims=True)
         eye = lax.broadcasted_iota(jnp.int32, (size, 128), 0) == lax.broadcasted_iota(
             jnp.int32, (size, 128), 1
@@ -271,6 +271,7 @@
             only(lax.rem(me + d, n) < owners, lambda d=d: [c.start() for c in scatter(d)] and None)
         for d in range(1, n):
             tell(d).start()
+        between()
 
         def reduce():
             total = part[me, :size]
@@ -299,11 +300,11 @@
             row += erecv[step, d - 1]
         return jnp.sum(jnp.where(eye, row[:1], 0.0), axis=1, keepdims=True)
 
-    def latent_layer(step, size):
-        energy_sum = exchange(step, size)
+    def latent_layer(step, size, between):
+        energy_sum = exchange(step, size, between)
         encoded = jnp.concatenate([gath[step, q, :size] for q in range(owners)], axis=1)
         active = jnp.tanh(dot(encoded, w_ref[...]) + bias_ref[...]).astype(BF16)
-        act_v[:size] = active
+        act_v[:size, :latent] = active
         base = jnp.concatenate([bgath[q] for q in range(owners)], axis=1)
         sums = scale * dot_t(active.astype(F32), base, precision=lax.Precision.HIGHEST)
         total, cross, quartic, square = grid_moments()
@@ -319,18 +320,18 @@
         mass_mult = (quartic * m[0] - cross * excess) / determinant
         energy_mult = (total * excess - cross * m[0]) / determinant / (grid * grid)
         values = [mass_mult] + [m[i] / (square * grid * grid) for i in (1, 2, 3)] + [energy_mult] * 2
-        lane = lax.broadcasted_iota(jnp.int32, (size, 2 * EXT), 1)
-        full = jnp.zeros((size, 2 * EXT), F32)
+        lane = lax.broadcasted_iota(jnp.int32, (size, 128), 1)
+        full = jnp.zeros((size, 128), F32)
         for i, value in enumerate(values):
-            full = jnp.where(lane % EXT == FIRST + i, -value, full)
+            full = jnp.where((lane % EXT == FIRST + i) & (lane < 2 * EXT), -value, full)
         high = full.astype(BF16).astype(F32)
-        mult[:size] = jnp.where(lane < EXT, high, full - high).astype(BF16)
-
-    def advanced(b, size):
+        act_v[:size, latent:] = jnp.where(lane < EXT, high, full - high).astype(BF16)
+
+    def advanced(b, size, active, mult):
         base = basis_ref[b]
-        collision = dot_t(act_v[:size], coder_v[b])
-        correction = dot(mult[:size], jnp.concatenate([base, base], axis=0))
-        return (f_v[b, :size] + correction + scale * collision).astype(BF16)
+        collision = dot_t(active, coder_v[b])
+        correction = dot(mult, jnp.concatenate([base] * (mult.shape[1] // EXT), axis=0))
+        return f_v[b, :size] + correction + scale * collision
 
     def courant(b):
         along = 2 * (blocks_ref[b] * WIDTH // (VGRID * VGRID)) + 1 - VGRID
@@ -393,34 +394,56 @@
                 acc[...] += dot(jnp.concatenate(parts, axis=1), coder_rows(start))
                 parts = []
 
-    latent_layer(0, rows)
+    def transported():
+        @pl.loop(0, count // unit)
+        def _(g):
+            for u in range(unit):
+                b = g * unit + u
+                f = f_v[b]
+                inflow = jnp.broadcast_to(inflow_ref[b], (EXT, WIDTH))
+                edge = jnp.where(keep > 0.0, f[cells:], inflow)
+                x = jnp.concatenate([f[:cells].astype(BF16), edge.astype(BF16)], axis=0)
+                weights = stencil(courant(b) * speed, second_ref[...])
+                f_v[b, :cells] = dot(weights, jnp.concatenate([x, x], axis=0))
+
+    latent_layer(0, rows, transported)
     zero()
-
-    @pl.loop(0, count // unit)
-    def _(g):
+    column = lax.broadcasted_iota(jnp.int32, (cells, rows), 1) - cells
+    shut = ((column >= 0) & (column < 2) & (jnp.full((cells, rows), open_left) == 0.0)) | (
+        (column >= 2) & (jnp.full((cells, rows), open_right) == 0.0)
+    )
+    inner = jnp.where(shut, 9.0, second_ref[...])
+    lanes = lax.broadcasted_iota(jnp.int32, (cells, 128), 1)
+
+    @pl.loop(0, chunks)
+    def _(c):
         parts = []
-        for u in range(unit):
-            b = g * unit + u
-            state = advanced(b, rows)
-            inflow = jnp.broadcast_to(inflow_ref[b], (EXT, WIDTH))
-            edge = jnp.where(keep > 0.0, state[cells:].astype(F32), inflow)
-            x = jnp.concatenate([state[:cells], edge.astype(BF16)], axis=0)
-            weights = stencil(courant(b) * speed, second_ref[...])
-            f = dot(weights, jnp.concatenate([x, x], axis=0))
+        for u in range(pack):
+            b = c * pack + u
+            held = act_v[...]
+            moved = dot(stencil(courant(b) * speed, inner), jnp.concatenate([held, held], axis=0))
+            mult = moved[:, latent:]
+            high = mult.astype(BF16).astype(F32)
+            low = pltpu.roll(mult - high, 2 * EXT, axis=1)
+            mult = jnp.where(lanes < 2 * EXT, high, low).astype(BF16)[:, : 4 * EXT]
+            f = advanced(b, cells, moved[:, :latent].astype(BF16), mult)
             f_v[b, :cells] = f
             eacc[:cells] += energy_of(f, b)
             parts.append(f.astype(BF16))
-        acc[:cells] += dot(jnp.concatenate(parts, axis=1), coder_rows(g * unit))
-
-    latent_layer(1, cells)
-
-    @pl.loop(0, count // unit)
-    def _(g):
-        for u in range(unit):
-            b = g * unit + u
-            p_v[b] = advanced(b, cells)
-        for u in range(unit):
-            out_copy(g * unit + u).start()
+            if len(parts) == unit:
+                acc[:cells] += dot(jnp.concatenate(parts, axis=1), coder_rows(b + 1 - unit))
+                parts = []
+
+    latent_layer(1, cells, lambda: None)
+
+    @pl.loop(0, chunks)
+    def _(c):
+        active = act_v[:cells, :latent]
+        mult = act_v[:cells, latent : latent + 2 * EXT]
+        for u in range(pack):
+            b = c * pack + u
+            p_v[b] = advanced(b, cells, active, mult).astype(BF16)
+            out_copy(b).start()
 
     @pl.loop(0, count)
     def _(b):
@@ -473,8 +496,7 @@
             pltpu.VMEM((2, 8, 128), F32),
             pltpu.VMEM((2, others, 8, 128), F32),
             pltpu.VMEM((owners, EXT, piece), F32),
-            pltpu.VMEM((rows, 2 * EXT), BF16),
-            pltpu.VMEM((rows, latent), BF16),
+            pltpu.VMEM((rows, latent + 128), BF16),
             dma((count,)), dma((count,)), dma((count,)),
             dma((2, others)), dma((2, others)), dma((2, others)), dma((2, owners)),
             dma((2, others)), dma((2, others)),

time: 82.7 us -> 78.6 us (0.950)
  Pallas kernels: 74.8 us -> 70.7 us
    pallas_call x1, Pallas kernels: 74.8 us -> 70.7 us  [body(): pl.pallas_call(functools.partial(kernel, n, owners, cells, math.sqrt(VELS...]
where the time goes in v5:
time: 78.6 us; the launch traced here: 78.5 us
  Pallas kernels  70.7 us (90%)
  local copies, waits for them, and re-layouts  7.76 us (10%)
    pallas_call x1, Pallas kernels, body(): pl.pallas_call(functools.partial(kernel, n, owners, cells, math.sqrt(VELS...  70.7 us
    unnamed x3, local copies, waits for them, and re-layouts  5.82 us

profile of v5, /device:TPU:0, one launch (start us, length us, event | category | flops | bytes accessed | tf_op | source)
XLA Modules:
  0.0 78.5 jit_solution(16126942503730648177)
XLA Ops:
  0.0 0.8 %slice_bitcast_fusion = (f32[1,2]{1,0:T(1,128)S(1)}, f32[1,2]{1,0:T(1,128)S(1)}) fusion(f32[96]{0:T(128)} %param.22), kind=kLoop, calls=%fused_computation | loop fusion | bytes 32 | tf_op jit(solution)/shard_map/reshape.59
  0.8 0.7 scatter.10
  1.5 0.2 scatter.11
  1.7 0.3 scatter.14.rest_ref
  1.9 0.0 copy-start
  2.0 0.6 copy-done
  2.5 70.7 %shard_map.118 = bf16[96,27648]{1,0:T(8,128)(2,1)} custom-call(s32[24]{0:T(128)} %blocks_ref.1, s32[4]{0:T(128)} %flags_ref.1, bf16[24,1152,512]{2,1,0:T(8,128)(2,1)} %bitcast.9, bf16[96,27648]{1,0:T(8,128)(2,1)} %dens_hbm.1, f32[112,128]{1,0:T(8,128)} %constant.93.clone.first_ref, f32[96,112]{1,0:T(8,128)} %constant.94.clone.second_ref, ...), custom_call_target="tpu_custom_call" | custom-call | flops 15854469120 | bytes 38928384 | tf_op jit(solution)/shard_map/pallas_call | solution.py:476
  73.2 5.2 %copy.16 = bf16[96,27648]{1,0:T(8,128)(2,1)} copy(bf16[96,27648]{1,0:T(8,128)(2,1)} %shard_map.118) | data formatting | bytes 10616832
Async XLA Ops:
  1.9 0.6 copy-start
